TPU v7x, 256 devices: a whole 4x4x8 slice. The times are simulated.
256 devices in a mesh: ctx: 32 (over y, x, z_lo), head: 8 (over z_hi, core).
Axes of the slice: x: 4, y: 4, z: 8 (z_hi: 4, z_lo: 2; z = z_hi * 2 + z_lo), core: 2. Of those that a mesh axis runs over, the one named last changes fastest.
Arguments:
- query: bfloat16 [8192, 16384], P('ctx', 'head'), may hold values from -42.5 to 42.5
- keys: bfloat16 [8192, 1024], P(('ctx', 'head')), may hold values from -6 to 6
- values: bfloat16 [8192, 1024], P(('ctx', 'head')), may hold values from -6 to 6
- d_out: bfloat16 [8192, 16384], P('ctx', 'head'), may hold values from -6 to 6
- lengths: int32 [16], replicated, may hold values from 1 to 8, as said below
Outputs:
- attn_out: bfloat16 [8192, 16384], P('ctx', 'head')
- d_query: bfloat16 [8192, 16384], P('ctx', 'head')
- d_keys: bfloat16 [8192, 1024], P(('ctx', 'head'))
- d_values: bfloat16 [8192, 1024], P(('ctx', 'head'))
Inputs may be any that keep to these rules, and one draw needn't show every extreme that they name: `lengths`: the documents lie in order from token 0 and together cover all 8192 tokens; one document has exactly 1024 tokens.
All inputs are finite; a program needn't handle non-finite values.
Results may differ from a plain program's by a relative error of at most 0.04.
Values may be sent and summed in bfloat16 or wider, within the bound.
A program may use at most 64 MiB of HBM per device.

v0:
```python
import math

import jax
import jax.numpy as jnp
from jax import lax
from jax.sharding import PartitionSpec as P

QH = 128
KVH = 8
DH = 128
BLK = 128
DOC_DEVS = 4


masked_score = -1e30


def shifted(value, axis, steps):
    count = lax.axis_size(axis)
    leading, last = (max(0, -steps), min(count, count - steps))
    return lax.ppermute(value, axis, [(source, source + steps) for source in range(leading, last)])


def document_ids(positions, doc_ends):
    return jnp.sum((positions[:, None] >= doc_ends[None, :]).astype(jnp.int32), axis=1)


def guarded(work, operand):
    result = work(operand)
    return result


def local(query, keys, values, d_out, lengths):
    tok_rows = query.shape[0]
    group_size = QH // KVH
    score_scale = 1.0 / math.sqrt(DH)
    keys_here, values_here = (
        lax.all_to_all(keys, "head", split_axis=1, concat_axis=0, tiled=True),
        lax.all_to_all(values, "head", split_axis=1, concat_axis=0, tiled=True),
    )
    kv_local = keys_here.shape[1] // DH
    query_heads = query.reshape(tok_rows, kv_local, group_size, DH)
    dout_heads = d_out.reshape(tok_rows, kv_local, group_size, DH)
    doc_ends = jnp.cumsum(lengths) * BLK
    ctx_place = lax.axis_index("ctx")
    offsets = jnp.arange(tok_rows, dtype=jnp.int32)
    query_pos = ctx_place * tok_rows + offsets
    query_doc = document_ids(query_pos, doc_ends)
    own_pair = jnp.stack((keys_here, values_here))
    pieces = [own_pair]
    current = own_pair
    for offset in range(DOC_DEVS):
        current = shifted(current, "ctx", 1)
        pieces.append(current)
    masks = []
    needs = []
    for offset in range(DOC_DEVS + 1):
        key_pos = (ctx_place - offset) * tok_rows + offsets
        key_doc = jnp.where(key_pos >= 0, document_ids(key_pos, doc_ends), -1)
        masks.append(
            (query_doc[:, None] == key_doc[None, :]) & (key_pos[None, :] <= query_pos[:, None])
        )
        needs.append(key_doc[tok_rows - 1] >= query_doc[0])

    def attend(kv_pair, allowed):
        key_rows = kv_pair[0].reshape(tok_rows, kv_local, DH)
        scores = (
            jnp.einsum("tkgd,skd->kgts", query_heads, key_rows, preferred_element_type=jnp.float32)
            * score_scale
        )
        return jnp.where(allowed[None, None], scores, masked_score)

    row_max = jnp.full((kv_local, group_size, tok_rows), masked_score, jnp.float32)
    row_sum = jnp.zeros((kv_local, group_size, tok_rows), jnp.float32)
    for offset in range(DOC_DEVS + 1):

        def update_stats(running, kv_pair=pieces[offset], allowed=masks[offset]):
            old_max, old_sum = running
            scores = attend(kv_pair, allowed)
            new_max = jnp.maximum(old_max, jnp.max(scores, axis=-1))
            new_sum = old_sum * jnp.exp(old_max - new_max) + jnp.sum(
                jnp.exp(scores - new_max[..., None]), axis=-1
            )
            return (new_max, new_sum)

        row_max, row_sum = guarded(update_stats, (row_max, row_sum))
    log_norm = row_max + jnp.log(row_sum)
    output_acc = jnp.zeros((tok_rows, kv_local, group_size, DH), jnp.float32)
    for offset in range(DOC_DEVS + 1):

        def add_output(running, kv_pair=pieces[offset], allowed=masks[offset]):
            value_rows = kv_pair[1].reshape(tok_rows, kv_local, DH)
            weights_low = jnp.exp(attend(kv_pair, allowed) - log_norm[..., None]).astype(
                jnp.bfloat16
            )
            return running + jnp.einsum(
                "kgts,skd->tkgd", weights_low, value_rows, preferred_element_type=jnp.float32
            )

        output_acc = guarded(add_output, output_acc)
    output_low = output_acc.astype(jnp.bfloat16)
    attn_out = output_low.reshape(tok_rows, kv_local * group_size * DH)
    row_delta = jnp.sum(
        dout_heads.astype(jnp.float32) * output_low.astype(jnp.float32), axis=-1
    ).transpose(1, 2, 0)
    grad_query = jnp.zeros((tok_rows, kv_local, group_size, DH), jnp.float32)
    partials = []
    for offset in range(DOC_DEVS + 1):

        def backward_piece(running, kv_pair=pieces[offset], allowed=masks[offset]):
            key_rows = kv_pair[0].reshape(tok_rows, kv_local, DH)
            value_rows = kv_pair[1].reshape(tok_rows, kv_local, DH)
            weights = jnp.exp(attend(kv_pair, allowed) - log_norm[..., None])
            weights_low = weights.astype(jnp.bfloat16)
            grad_probs = jnp.einsum(
                "tkgd,skd->kgts", dout_heads, value_rows, preferred_element_type=jnp.float32
            )
            grad_scores = (weights * (grad_probs - row_delta[..., None])).astype(jnp.bfloat16)
            new_query = running + jnp.einsum(
                "kgts,skd->tkgd", grad_scores, key_rows, preferred_element_type=jnp.float32
            )
            grad_keys = (
                jnp.einsum(
                    "kgts,tkgd->skd", grad_scores, query_heads, preferred_element_type=jnp.float32
                )
                * score_scale
            )
            grad_values = jnp.einsum(
                "kgts,tkgd->skd", weights_low, dout_heads, preferred_element_type=jnp.float32
            )
            stacked = jnp.stack((grad_keys, grad_values)).reshape(2, tok_rows, kv_local * DH)
            return (new_query, stacked)

        grad_query, stacked = guarded(backward_piece, grad_query)
        partials.append(stacked)
    d_query = (
        (grad_query * score_scale)
        .astype(jnp.bfloat16)
        .reshape(tok_rows, kv_local * group_size * DH)
    )
    carried = partials[DOC_DEVS]
    for offset in range(DOC_DEVS, 0, -1):
        carried = shifted(carried, "ctx", -1)
        carried = carried + partials[offset - 1]
    grad_low = carried.astype(jnp.bfloat16)
    d_keys, d_values = (
        lax.all_to_all(grad_low[0], "head", split_axis=0, concat_axis=1, tiled=True),
        lax.all_to_all(grad_low[1], "head", split_axis=0, concat_axis=1, tiled=True),
    )
    return (attn_out, d_query, d_keys, d_values)


def solution(mesh):
    in_specs = (
        P("ctx", "head"),
        P(("ctx", "head"), None),
        P(("ctx", "head"), None),
        P("ctx", "head"),
        P(),
    )
    out_specs = (
        P("ctx", "head"),
        P("ctx", "head"),
        P(("ctx", "head"), None),
        P(("ctx", "head"), None),
    )
    return jax.shard_map(local, mesh=mesh, in_specs=in_specs, out_specs=out_specs, check_vma=False)
```

profile of v0, /device:TPU:38, one launch (start us, length us, event | category | flops | bytes accessed | tf_op | source)
XLA Modules:
  0.0 171.7 jit_solution(14606386016077690862)
XLA Ops:
  0.6 1.6 copy_bitcast_fusion.3
  2.2 7.6 %all-to-all-start = ((bf16[32,8,128]{2,0,1:T(8,128)(2,1)}), bf16[32,8,128]{2,0,1:T(8,128)(2,1)S(1)}, u32[]{:S(2)}, u32[]{:S(2)}) async-start(bf16[32,8,128]{2,0,1:T(8,128)(2,1)} %copy_bitcast_fusion.3), calls=%async_computation | async-start | bytes 131072 | tf_op jit(solution)/shard_map/all_to_all | solution.py:38
  10.7 1.5 copy_bitcast_fusion.2
  12.4 5.8 %all-to-all-done = bf16[32,8,128]{2,0,1:T(8,128)(2,1)S(1)} async-done(((bf16[32,8,128]{2,0,1:T(8,128)(2,1)}), bf16[32,8,128]{2,0,1:T(8,128)(2,1)S(1)}, u32[]{:S(2)}, u32[]{:S(2)}) %all-to-all-start) | async-done | bytes 65568 | tf_op jit(solution)/shard_map/all_to_all | solution.py:38
  18.1 4.0 %all-to-all-start.1 = ((bf16[32,8,128]{2,0,1:T(8,128)(2,1)}), bf16[32,8,128]{2,0,1:T(8,128)(2,1)}, u32[]{:S(2)}, u32[]{:S(2)}) async-start(bf16[32,8,128]{2,0,1:T(8,128)(2,1)} %copy_bitcast_fusion.2), calls=%async_computation.1 | async-start | bytes 131072 | tf_op jit(solution)/shard_map/all_to_all | solution.py:39
  22.7 1.5 copy.221
  24.2 6.3 %all-to-all-done.1 = bf16[32,8,128]{2,0,1:T(8,128)(2,1)} async-done(((bf16[32,8,128]{2,0,1:T(8,128)(2,1)}), bf16[32,8,128]{2,0,1:T(8,128)(2,1)}, u32[]{:S(2)}, u32[]{:S(2)}) %all-to-all-start.1) | async-done | bytes 65568 | tf_op jit(solution)/shard_map/all_to_all | solution.py:39
  31.4 3.8 %collective-permute-start = (bf16[2,256,128]{2,1,0:T(8,128)(2,1)S(1)}, bf16[2,256,128]{2,1,0:T(8,128)(2,1)S(1)}, u32[]{:S(2)}, u32[]{:S(2)}) collective-permute-start(bf16[2,256,128]{2,1,0:T(8,128)(2,1)S(1)} %pad_maximum_fusion), channel_id=1, source_target_pairs={{0,8},{8,16},{16,24},{24,32},{32,40},{40,48},{48,56},{56,64},{64,7... | collective-permute-start | bytes 393224 | tf_op jit(solution)/shard_map/ppermute | solution.py:21
  36.0 2.4 %collective-permute-done = bf16[2,256,128]{2,1,0:T(8,128)(2,1)S(1)} collective-permute-done((bf16[2,256,128]{2,1,0:T(8,128)(2,1)S(1)}, bf16[2,256,128]{2,1,0:T(8,128)(2,1)S(1)}, u32[]{:S(2)}, u32[]{:S(2)}) %collective-permute-start) | collective-permute-done | bytes 131104 | tf_op jit(solution)/shard_map/ppermute | solution.py:21
  38.4 6.8 %collective-permute-start.1 = (bf16[2,256,128]{2,1,0:T(8,128)(2,1)S(1)}, bf16[2,256,128]{2,1,0:T(8,128)(2,1)S(1)}, u32[]{:S(2)}, u32[]{:S(2)}) collective-permute-start(bf16[2,256,128]{2,1,0:T(8,128)(2,1)S(1)} %collective-permute-done), channel_id=1, source_target_pairs={{0,8},{8,16},{16,24},{24,32},{32,40},{40,48},{48,56},{56,64},{64,7... | collective-permute-start | bytes 393224 | tf_op jit(solution)/shard_map/ppermute | solution.py:21
  46.0 1.7 collective-permute-done.1
  47.7 7.4 %collective-permute-start.2 = (bf16[2,256,128]{2,1,0:T(8,128)(2,1)S(1)}, bf16[2,256,128]{2,1,0:T(8,128)(2,1)S(1)}, u32[]{:S(2)}, u32[]{:S(2)}) collective-permute-start(bf16[2,256,128]{2,1,0:T(8,128)(2,1)S(1)} %collective-permute-done.1), channel_id=1, source_target_pairs={{0,8},{8,16},{16,24},{24,32},{32,40},{40,48},{48,56},{56,64},{64,7... | collective-permute-start | bytes 393224 | tf_op jit(solution)/shard_map/ppermute | solution.py:21
  55.9 1.7 collective-permute-done.2
  57.6 7.5 %collective-permute-start.3 = (bf16[2,256,128]{2,1,0:T(8,128)(2,1)S(1)}, bf16[2,256,128]{2,1,0:T(8,128)(2,1)S(1)}, u32[]{:S(2)}, u32[]{:S(2)}) collective-permute-start(bf16[2,256,128]{2,1,0:T(8,128)(2,1)S(1)} %collective-permute-done.2), channel_id=1, source_target_pairs={{0,8},{8,16},{16,24},{24,32},{32,40},{40,48},{48,56},{56,64},{64,7... | collective-permute-start | bytes 393224 | tf_op jit(solution)/shard_map/ppermute | solution.py:21
  65.9 1.5 collective-permute-done.3
  68.3 0.9 exponential_reduce_fusion.4
  69.2 0.9 exponential_reduce_fusion.3
  72.8 1.3 convolution_bitcast_fusion.4
  74.1 1.3 convolution_bitcast_fusion.3
  75.4 1.9 %convolution_bitcast_fusion.2 = f32[1,256,1,128]{3,1,2,0:T(8,128)} fusion(f32[256,256,16]{1,0,2:T(8,128)S(1)} %get-tuple-element.46, f32[16,256]{1,0:T(8,128)S(1)} %log_add_fusion, pred[256,256]{0,1:T(8,128)(4,1)S(1)} %get-tuple-element.40, bf16[256,2048]{1,0:T(8,128)(2,1)S(1)} %copy-done.2), kind=kOutput, calls=%fused_computation.84 | convolution fusion | flops 272629760 | bytes 5455872 | tf_op jit(solution)/shard_map/kgts,tkgd->skd/dot_general | solution.py:128
  77.3 1.9 %convolution_bitcast_fusion.1 = f32[1,256,1,128]{3,1,2,0:T(8,128)} fusion(f32[256,256,16]{1,0,2:T(8,128)S(1)} %get-tuple-element.48, f32[16,256]{1,0:T(8,128)S(1)} %log_add_fusion, pred[256,256]{0,1:T(8,128)(4,1)S(1)} %get-tuple-element.39, bf16[256,2048]{1,0:T(8,128)(2,1)S(1)} %copy-done.2), kind=kOutput, calls=%fused_computation.83 | convolution fusion | flops 272629760 | bytes 5455872 | tf_op jit(solution)/shard_map/kgts,tkgd->skd/dot_general | solution.py:128
  79.2 2.1 %convolution_bitcast_fusion = f32[1,256,1,128]{3,1,0,2:T(8,128)} fusion(f32[256,256,16]{1,0,2:T(8,128)S(1)} %get-tuple-element.50, f32[16,256]{1,0:T(8,128)S(1)} %log_add_fusion, pred[256,256]{0,1:T(8,128)(4,1)S(1)} %get-tuple-element.36, bf16[256,2048]{1,0:T(8,128)(2,1)S(1)} %copy-done.2), kind=kOutput, calls=%fused_computation.82 | convolution fusion | flops 272629760 | bytes 5455872 | tf_op jit(solution)/shard_map/kgts,tkgd->skd/dot_general | solution.py:128
  81.4 1.9 %fusion.135 = f32[16,256,128]{1,2,0:T(8,128)S(1)} fusion(bf16[256,128,1]{1,0,2:T(8,128)(2,1)} %bitcast.27, f32[256,256,16]{1,0,2:T(8,128)S(1)} %get-tuple-element.50, f32[16,256]{1,0:T(8,128)S(1)} %log_add_fusion, pred[256,256]{0,1:T(8,128)(4,1)S(1)} %get-tuple-element.36), kind=kOutput, calls=%fused_computation.159 | convolution fusion | flops 272629760 | bytes 6438912 | tf_op jit(solution)/shard_map/kgts,skd->tkgd/dot_general | solution.py:96
  83.3 1.2 fusion.131
  84.5 1.2 fusion.132
  85.7 1.2 fusion.133
  86.8 2.8 %multiply_reduce_fusion = (f32[256,16]{0,1:T(8,128)S(1)}, bf16[128,16,256]{2,0,1:T(8,128)(2,1)}) fusion(f32[256,1,16,128]{0,3,2,1:T(8,128)S(1)} %bitcast.605, f32[256,256,16]{1,0,2:T(8,128)S(1)} %get-tuple-element.42, f32[16,256]{1,0:T(8,128)S(1)} %log_add_fusion, pred[256,256]{0,1:T(8,128)(4,1)S(1)} %get-tuple-element.38, ...), kind=kOutput, calls=%fused_computation.76 | convolution fusion | flops 276819968 | bytes 15892480 | tf_op jit(solution)/shard_map/kgts,skd->tkgd/dot_general | solution.py:96
  89.7 2.3 %fusion.9 = bf16[1,16,256,256]{2,3,1,0:T(8,128)(2,1)S(1)} fusion(f32[256,256,16]{1,0,2:T(8,128)S(1)} %get-tuple-element.50, bf16[256,128,1]{1,0,2:T(8,128)(2,1)} %bitcast.27, f32[16,256]{1,0:T(8,128)S(1)} %bitcast.611, f32[16,256]{1,0:T(8,128)S(1)} %log_add_fusion, pred[256,256]{0,1:T(8,128)(4,1)S(1)} %get-tuple-element.36, bf16[256,2048]{1,0:T(8,128)(2,1)S(1)} %copy-done.2), kind=kOutput, calls=%fused_computation.14 | convolution fusion | flops 274726912 | bytes 7503872 | tf_op jit(solution)/shard_map/tkgd,skd->kgts/dot_general | solution.py:115
  92.0 1.5 fusion.1
  94.2 2.2 %collective-permute-start.4 = (f32[2,256,128]{2,1,0:T(8,128)S(1)}, f32[2,256,128]{2,1,0:T(8,128)S(1)}, u32[]{:S(2)}, u32[]{:S(2)}) collective-permute-start(f32[2,256,128]{2,1,0:T(8,128)S(1)} %maximum_bitcast_fusion), channel_id=1, source_target_pairs={{8,0},{16,8},{24,16},{32,24},{40,32},{48,40},{56,48},{64,56},{72,6... | collective-permute-start | bytes 786440 | tf_op jit(solution)/shard_map/ppermute | solution.py:21
  96.9 1.5 fusion.3
  98.3 1.5 fusion.5
  99.8 1.5 fusion.7
  101.3 1.8 %fusion.39 = f32[128,16,256]{2,0,1:T(8,128)} fusion(bf16[1,16,256,256]{2,3,1,0:T(8,128)(2,1)S(1)} %fusion.7, bf16[2,256,128]{2,1,0:T(8,128)(2,1)S(1)} %collective-permute-done), kind=kOutput, calls=%fused_computation.59 | convolution fusion | flops 268435456 | bytes 4259840 | tf_op jit(solution)/shard_map/kgts,skd->tkgd/dot_general | solution.py:119
  103.1 1.8 %fusion.35 = f32[128,16,256]{2,0,1:T(8,128)} fusion(bf16[1,16,256,256]{2,3,1,0:T(8,128)(2,1)S(1)} %fusion.5, bf16[2,256,128]{2,1,0:T(8,128)(2,1)S(1)} %collective-permute-done.1), kind=kOutput, calls=%fused_computation.55 | convolution fusion | flops 268435456 | bytes 4259840 | tf_op jit(solution)/shard_map/kgts,skd->tkgd/dot_general | solution.py:119
  104.9 1.8 %fusion.31 = f32[128,16,256]{2,0,1:T(8,128)} fusion(bf16[1,16,256,256]{2,3,1,0:T(8,128)(2,1)S(1)} %fusion.3, bf16[2,256,128]{2,1,0:T(8,128)(2,1)S(1)} %collective-permute-done.2), kind=kOutput, calls=%fused_computation.51 | convolution fusion | flops 268435456 | bytes 4259840 | tf_op jit(solution)/shard_map/kgts,skd->tkgd/dot_general | solution.py:119
  107.4 1.9 %collective-permute-start.5 = (f32[2,256,128]{2,1,0:T(8,128)S(1)}, f32[2,256,128]{2,1,0:T(8,128)S(1)}, u32[]{:S(2)}, u32[]{:S(2)}) collective-permute-start(f32[2,256,128]{2,1,0:T(8,128)S(1)} %fusion.126), channel_id=1, source_target_pairs={{8,0},{16,8},{24,16},{32,24},{40,32},{48,40},{56,48},{64,56},{72,6... | collective-permute-start | bytes 786440 | tf_op jit(solution)/shard_map/ppermute | solution.py:21
  110.1 9.0 %collective-permute-done.5 = f32[2,256,128]{2,1,0:T(8,128)S(1)} collective-permute-done((f32[2,256,128]{2,1,0:T(8,128)S(1)}, f32[2,256,128]{2,1,0:T(8,128)S(1)}, u32[]{:S(2)}, u32[]{:S(2)}) %collective-permute-start.5) | collective-permute-done | bytes 262176 | tf_op jit(solution)/shard_map/ppermute | solution.py:21
  119.2 2.1 %collective-permute-start.6 = (f32[2,256,128]{2,1,0:T(8,128)S(1)}, f32[2,256,128]{2,1,0:T(8,128)S(1)}, u32[]{:S(2)}, u32[]{:S(2)}) collective-permute-start(f32[2,256,128]{2,1,0:T(8,128)S(1)} %fusion.127), channel_id=1, source_target_pairs={{8,0},{16,8},{24,16},{32,24},{40,32},{48,40},{56,48},{64,56},{72,6... | collective-permute-start | bytes 786440 | tf_op jit(solution)/shard_map/ppermute | solution.py:21
  122.0 8.6 %collective-permute-done.6 = f32[2,256,128]{2,1,0:T(8,128)S(1)} collective-permute-done((f32[2,256,128]{2,1,0:T(8,128)S(1)}, f32[2,256,128]{2,1,0:T(8,128)S(1)}, u32[]{:S(2)}, u32[]{:S(2)}) %collective-permute-start.6) | collective-permute-done | bytes 262176 | tf_op jit(solution)/shard_map/ppermute | solution.py:21
  130.7 1.9 %collective-permute-start.7 = (f32[2,256,128]{2,1,0:T(8,128)S(1)}, f32[2,256,128]{2,1,0:T(8,128)S(1)}, u32[]{:S(2)}, u32[]{:S(2)}) collective-permute-start(f32[2,256,128]{2,1,0:T(8,128)S(1)} %fusion.128), channel_id=1, source_target_pairs={{8,0},{16,8},{24,16},{32,24},{40,32},{48,40},{56,48},{64,56},{72,6... | collective-permute-start | bytes 786440 | tf_op jit(solution)/shard_map/ppermute | solution.py:21
  133.3 8.6 %collective-permute-done.7 = f32[2,256,128]{2,1,0:T(8,128)S(1)} collective-permute-done((f32[2,256,128]{2,1,0:T(8,128)S(1)}, f32[2,256,128]{2,1,0:T(8,128)S(1)}, u32[]{:S(2)}, u32[]{:S(2)}) %collective-permute-start.7) | collective-permute-done | bytes 262176 | tf_op jit(solution)/shard_map/ppermute | solution.py:21
  142.6 3.4 %all-to-all-start.3 = ((bf16[8,32,128]{2,1,0:T(8,128)(2,1)}), bf16[8,32,128]{2,1,0:T(8,128)(2,1)S(1)}, u32[]{:S(2)}, u32[]{:S(2)}) async-start(bf16[8,32,128]{2,1,0:T(8,128)(2,1)} %bitcast.137), calls=%async_computation.3 | async-start | bytes 131072 | tf_op jit(solution)/shard_map/all_to_all | solution.py:148
  146.0 5.2 %fusion.45 = bf16[128,16,256]{2,0,1:T(8,128)(2,1)} fusion(f32[128,16,256]{2,0,1:T(8,128)} %fusion.31, f32[128,16,256]{2,0,1:T(8,128)} %fusion.35, f32[128,16,256]{2,0,1:T(8,128)} %fusion.39, f32[16,256,128]{1,2,0:T(8,128)S(1)} %fusion.48, bf16[1,16,256,256]{2,3,1,0:T(8,128)(2,1)} %copy-done.1, bf16[2,256,128]{2,1,0:T(8,128)(2,1)S(1)} %copy-done.4), kind=kOutput, calls=%fused_computation.66 | convolution fusion | flops 271581184 | bytes 11599872 | tf_op jit(solution)/shard_map/kgts,skd->tkgd/dot_general | solution.py:119
  151.2 2.3 %copy.249 = bf16[256,2048]{1,0:T(8,128)(2,1)} copy(bf16[256,2048]{0,1:T(8,128)(2,1)} %bitcast.606) | data formatting | bytes 2097152
  153.5 2.3 %copy.248 = bf16[256,2048]{1,0:T(8,128)(2,1)} copy(bf16[256,2048]{0,1:T(8,128)(2,1)} %bitcast.607) | data formatting | bytes 2097152
  155.8 7.1 %all-to-all-start.2 = ((bf16[8,32,128]{2,1,0:T(8,128)(2,1)}), bf16[8,32,128]{2,1,0:T(8,128)(2,1)S(1)}, u32[]{:S(2)}, u32[]{:S(2)}) async-start(bf16[8,32,128]{2,1,0:T(8,128)(2,1)} %bitcast.135), calls=%async_computation.2 | async-start | bytes 131072 | tf_op jit(solution)/shard_map/all_to_all | solution.py:147
  163.5 7.6 %all-to-all-done.2 = bf16[8,32,128]{2,1,0:T(8,128)(2,1)S(1)} async-done(((bf16[8,32,128]{2,1,0:T(8,128)(2,1)}), bf16[8,32,128]{2,1,0:T(8,128)(2,1)S(1)}, u32[]{:S(2)}, u32[]{:S(2)}) %all-to-all-start.2) | async-done | bytes 65568 | tf_op jit(solution)/shard_map/all_to_all | solution.py:147
  (56 shorter events, 15.5 us)
Async XLA Ops:
  0.6 34.6 %copy-start = (bf16[256,2048]{1,0:T(8,128)(2,1)S(1)}, bf16[256,2048]{1,0:T(8,128)(2,1)}, u32[]{:S(2)}) copy-start(bf16[256,2048]{1,0:T(8,128)(2,1)} %param.5) | copy-start | bytes 3145732
  2.2 15.9 %all-to-all-start = ((bf16[32,8,128]{2,0,1:T(8,128)(2,1)}), bf16[32,8,128]{2,0,1:T(8,128)(2,1)S(1)}, u32[]{:S(2)}, u32[]{:S(2)}) async-start(bf16[32,8,128]{2,0,1:T(8,128)(2,1)} %copy_bitcast_fusion.3), calls=%async_computation | async-start | bytes 131072 | tf_op jit(solution)/shard_map/all_to_all | solution.py:38
  18.1 12.4 %all-to-all-start.1 = ((bf16[32,8,128]{2,0,1:T(8,128)(2,1)}), bf16[32,8,128]{2,0,1:T(8,128)(2,1)}, u32[]{:S(2)}, u32[]{:S(2)}) async-start(bf16[32,8,128]{2,0,1:T(8,128)(2,1)} %copy_bitcast_fusion.2), calls=%async_computation.1 | async-start | bytes 131072 | tf_op jit(solution)/shard_map/all_to_all | solution.py:39
  31.4 7.0 %collective-permute-start = (bf16[2,256,128]{2,1,0:T(8,128)(2,1)S(1)}, bf16[2,256,128]{2,1,0:T(8,128)(2,1)S(1)}, u32[]{:S(2)}, u32[]{:S(2)}) collective-permute-start(bf16[2,256,128]{2,1,0:T(8,128)(2,1)S(1)} %pad_maximum_fusion), channel_id=1, source_target_pairs={{0,8},{8,16},{16,24},{24,32},{32,40},{40,48},{48,56},{56,64},{64,7... | collective-permute-start | bytes 393224 | tf_op jit(solution)/shard_map/ppermute | solution.py:21
  38.4 9.3 %collective-permute-start.1 = (bf16[2,256,128]{2,1,0:T(8,128)(2,1)S(1)}, bf16[2,256,128]{2,1,0:T(8,128)(2,1)S(1)}, u32[]{:S(2)}, u32[]{:S(2)}) collective-permute-start(bf16[2,256,128]{2,1,0:T(8,128)(2,1)S(1)} %collective-permute-done), channel_id=1, source_target_pairs={{0,8},{8,16},{16,24},{24,32},{32,40},{40,48},{48,56},{56,64},{64,7... | collective-permute-start | bytes 393224 | tf_op jit(solution)/shard_map/ppermute | solution.py:21
  47.7 9.9 %collective-permute-start.2 = (bf16[2,256,128]{2,1,0:T(8,128)(2,1)S(1)}, bf16[2,256,128]{2,1,0:T(8,128)(2,1)S(1)}, u32[]{:S(2)}, u32[]{:S(2)}) collective-permute-start(bf16[2,256,128]{2,1,0:T(8,128)(2,1)S(1)} %collective-permute-done.1), channel_id=1, source_target_pairs={{0,8},{8,16},{16,24},{24,32},{32,40},{40,48},{48,56},{56,64},{64,7... | collective-permute-start | bytes 393224 | tf_op jit(solution)/shard_map/ppermute | solution.py:21
  57.6 9.9 %collective-permute-start.3 = (bf16[2,256,128]{2,1,0:T(8,128)(2,1)S(1)}, bf16[2,256,128]{2,1,0:T(8,128)(2,1)S(1)}, u32[]{:S(2)}, u32[]{:S(2)}) collective-permute-start(bf16[2,256,128]{2,1,0:T(8,128)(2,1)S(1)} %collective-permute-done.2), channel_id=1, source_target_pairs={{0,8},{8,16},{16,24},{24,32},{32,40},{40,48},{48,56},{56,64},{64,7... | collective-permute-start | bytes 393224 | tf_op jit(solution)/shard_map/ppermute | solution.py:21
  67.4 24.5 %copy-start.3 = (bf16[2,256,128]{2,1,0:T(8,128)(2,1)}, bf16[2,256,128]{2,1,0:T(8,128)(2,1)S(1)}, u32[]{:S(2)}) copy-start(bf16[2,256,128]{2,1,0:T(8,128)(2,1)S(1)} %collective-permute-done.3) | copy-start | bytes 393220
  71.0 1.8 %copy-start.2 = (bf16[256,2048]{1,0:T(8,128)(2,1)S(1)}, bf16[256,2048]{1,0:T(8,128)(2,1)}, u32[]{:S(2)}) copy-start(bf16[256,2048]{1,0:T(8,128)(2,1)} %param.8) | copy-start | bytes 3145732
  93.4 2.9 %copy-start.1 = (bf16[1,16,256,256]{2,3,1,0:T(8,128)(2,1)}, bf16[1,16,256,256]{2,3,1,0:T(8,128)(2,1)S(1)}, u32[]{:S(2)}) copy-start(bf16[1,16,256,256]{2,3,1,0:T(8,128)(2,1)S(1)} %fusion.1) | copy-start | bytes 6291460
  94.2 13.2 %collective-permute-start.4 = (f32[2,256,128]{2,1,0:T(8,128)S(1)}, f32[2,256,128]{2,1,0:T(8,128)S(1)}, u32[]{:S(2)}, u32[]{:S(2)}) collective-permute-start(f32[2,256,128]{2,1,0:T(8,128)S(1)} %maximum_bitcast_fusion), channel_id=1, source_target_pairs={{8,0},{16,8},{24,16},{32,24},{40,32},{48,40},{56,48},{64,56},{72,6... | collective-permute-start | bytes 786440 | tf_op jit(solution)/shard_map/ppermute | solution.py:21
  106.7 12.5 %copy-start.7 = (f32[1,256,1,128]{3,1,2,0:T(8,128)S(1)}, f32[1,256,1,128]{3,1,2,0:T(8,128)}, u32[]{:S(2)}) copy-start(f32[1,256,1,128]{3,1,2,0:T(8,128)} %convolution_bitcast_fusion.2) | copy-start | bytes 393220
  107.4 23.2 %copy-start.6 = (f32[1,256,1,128]{3,1,2,0:T(8,128)S(1)}, f32[1,256,1,128]{3,1,2,0:T(8,128)}, u32[]{:S(2)}) copy-start(f32[1,256,1,128]{3,1,2,0:T(8,128)} %convolution_bitcast_fusion.1) | copy-start | bytes 393220
  107.4 11.7 %collective-permute-start.5 = (f32[2,256,128]{2,1,0:T(8,128)S(1)}, f32[2,256,128]{2,1,0:T(8,128)S(1)}, u32[]{:S(2)}, u32[]{:S(2)}) collective-permute-start(f32[2,256,128]{2,1,0:T(8,128)S(1)} %fusion.126), channel_id=1, source_target_pairs={{8,0},{16,8},{24,16},{32,24},{40,32},{48,40},{56,48},{64,56},{72,6... | collective-permute-start | bytes 786440 | tf_op jit(solution)/shard_map/ppermute | solution.py:21
  110.1 31.8 %copy-start.5 = (f32[1,256,1,128]{3,1,0,2:T(8,128)S(1)}, f32[1,256,1,128]{3,1,0,2:T(8,128)}, u32[]{:S(2)}) copy-start(f32[1,256,1,128]{3,1,0,2:T(8,128)} %convolution_bitcast_fusion) | copy-start | bytes 393220
  119.2 26.8 %copy-start.4 = (bf16[2,256,128]{2,1,0:T(8,128)(2,1)S(1)}, bf16[2,256,128]{2,1,0:T(8,128)(2,1)}, u32[]{:S(2)}) copy-start(bf16[2,256,128]{2,1,0:T(8,128)(2,1)} %copy-done.3) | copy-start | bytes 393220
  119.2 11.4 %collective-permute-start.6 = (f32[2,256,128]{2,1,0:T(8,128)S(1)}, f32[2,256,128]{2,1,0:T(8,128)S(1)}, u32[]{:S(2)}, u32[]{:S(2)}) collective-permute-start(f32[2,256,128]{2,1,0:T(8,128)S(1)} %fusion.127), channel_id=1, source_target_pairs={{8,0},{16,8},{24,16},{32,24},{40,32},{48,40},{56,48},{64,56},{72,6... | collective-permute-start | bytes 786440 | tf_op jit(solution)/shard_map/ppermute | solution.py:21
  130.7 11.3 %collective-permute-start.7 = (f32[2,256,128]{2,1,0:T(8,128)S(1)}, f32[2,256,128]{2,1,0:T(8,128)S(1)}, u32[]{:S(2)}, u32[]{:S(2)}) collective-permute-start(f32[2,256,128]{2,1,0:T(8,128)S(1)} %fusion.128), channel_id=1, source_target_pairs={{8,0},{16,8},{24,16},{32,24},{40,32},{48,40},{56,48},{64,56},{72,6... | collective-permute-start | bytes 786440 | tf_op jit(solution)/shard_map/ppermute | solution.py:21
  142.6 13.1 %all-to-all-start.3 = ((bf16[8,32,128]{2,1,0:T(8,128)(2,1)}), bf16[8,32,128]{2,1,0:T(8,128)(2,1)S(1)}, u32[]{:S(2)}, u32[]{:S(2)}) async-start(bf16[8,32,128]{2,1,0:T(8,128)(2,1)} %bitcast.137), calls=%async_computation.3 | async-start | bytes 131072 | tf_op jit(solution)/shard_map/all_to_all | solution.py:148
  155.8 15.3 %all-to-all-start.2 = ((bf16[8,32,128]{2,1,0:T(8,128)(2,1)}), bf16[8,32,128]{2,1,0:T(8,128)(2,1)S(1)}, u32[]{:S(2)}, u32[]{:S(2)}) async-start(bf16[8,32,128]{2,1,0:T(8,128)(2,1)} %bitcast.135), calls=%async_computation.2 | async-start | bytes 131072 | tf_op jit(solution)/shard_map/all_to_all | solution.py:147
where the time goes:
time: 173 us; the launch traced here: 172 us
  starting transfers between devices  55.6 us (32%)
  waiting for transfers between devices  53.1 us (31%)
  matrix products  43.8 us (25%)
  local copies, waits for them, and re-layouts  11.8 us (7%)
  other arithmetic  6.32 us (4%)
    ppermute x8, starting transfers between devices, shifted(): lax.ppermute(value, axis, [(source, source + steps) for source in range(l...  33.6 us
    ppermute x8, waiting for transfers between devices, shifted(): lax.ppermute(value, axis, [(source, source + steps) for source in range(l...  33.4 us
    dot_general x5, matrix products, backward_piece(): jnp.einsum('kgts,skd->tkgd', grad_scores, key_rows, preferred_element_typ...  11.1 us
    dot_general x5, matrix products, backward_piece(): jnp.einsum('kgts,tkgd->skd', weights_low, dout_heads, preferred_element_t...  8.54 us
    dot_general x5, matrix products, add_output(): jnp.einsum('kgts,skd->tkgd', weights_low, value_rows, preferred_element_t...  8.26 us
    dot_general x5, matrix products, backward_piece(): jnp.einsum('tkgd,skd->kgts', dout_heads, value_rows, preferred_element_ty...  8.14 us
    all_to_all x1, waiting for transfers between devices, local(): lax.all_to_all(grad_low[0], 'head', split_axis=0, concat_axis=1, tiled=True)  7.58 us
    all_to_all x1, starting transfers between devices, local(): lax.all_to_all(keys, 'head', split_axis=1, concat_axis=0, tiled=True)  7.57 us
  transfers between devices with their start and end apart: 12, of which 10 were waited for; matrix products, arithmetic and copies ran while one was open for 18% of the time, Pallas kernels for 0%

commit v1 on v0

v1 whole, which is shorter than its diff:
```python
import functools
import math

import jax
import jax.numpy as jnp
from jax import lax
from jax.experimental import pallas as pl
from jax.experimental.pallas import tpu as pltpu
from jax.sharding import PartitionSpec as P

QH = 128
KVH = 8
DH = 128
BLK = 128
GROUP = QH // KVH
PAIRS = GROUP // 2
MESH = pl.DeviceIdType.MESH
BF = jnp.bfloat16
F32 = jnp.float32
SCALE = 1.0 / math.sqrt(DH)
C2 = SCALE * math.log2(math.e)
MASKED = -1e30


def dot(a, b):
    return lax.dot_general(a, b, (((1,), (0,)), ((), ())), preferred_element_type=F32)


def kernel(
    n_ctx, n_head,
    len_ref, q_hbm, k_hbm, v_hbm, do_hbm,
    o_hbm, dq_hbm, dk_ref, dv_ref,
    q_ref, do_ref, k_ref, v_ref, qt, dot_t, kv, kk, vv, kt, vte, tri,
    m_run, m_tile, acc, p_all, dp_all, dqt, dk_acc, dv_acc,
    o_out, dq_out, gsend, grecv, gown, gfin, stage,
    load_sem, out_sem, a_send, a_recv, c_send, c_recv, g_send, g_recv, b_send, b_recv,
):
    c = lax.axis_index("ctx")
    h = lax.axis_index("head")

    def peer(j):
        return (c, lax.rem(h + j, n_head))

    def after(o):
        return (lax.rem(c + o, n_ctx), h)

    def before(o):
        return (lax.rem(c + n_ctx - o, n_ctx), h)

    loads = [
        pltpu.make_async_copy(k_hbm, k_ref, load_sem.at[0]),
        pltpu.make_async_copy(v_hbm, v_ref, load_sem.at[1]),
        pltpu.make_async_copy(q_hbm, q_ref, load_sem.at[2]),
        pltpu.make_async_copy(do_hbm, do_ref, load_sem.at[3]),
    ]
    for copy in loads:
        copy.start()

    barrier = pltpu.get_barrier_semaphore()
    for j in range(1, n_head):
        pl.semaphore_signal(barrier, inc=1, device_id=peer(j), device_id_type=MESH)
    for o in range(1, 5):
        pl.semaphore_signal(barrier, inc=1, device_id=after(o), device_id_type=MESH)
        pl.semaphore_signal(barrier, inc=1, device_id=before(o), device_id_type=MESH)

    loads[0].wait()
    loads[1].wait()
    for j in range(n_head):
        stage[j, 0] = k_ref[:, j * DH:(j + 1) * DH]
        stage[j, 1] = v_ref[:, j * DH:(j + 1) * DH]
    kv[0, h] = stage[h]
    pl.semaphore_wait(barrier, n_head - 1 + 8)

    heads_in = []
    for j in range(1, n_head):
        copy = pltpu.make_async_remote_copy(
            src_ref=stage.at[lax.rem(h + j, n_head)], dst_ref=kv.at[0, h],
            send_sem=a_send.at[j - 1], recv_sem=a_recv.at[j - 1],
            device_id=peer(j), device_id_type=MESH)
        copy.start()
        heads_in.append(copy)

    loads[2].wait()
    loads[3].wait()

    def transpose_pair(i, carry):
        u = i // PAIRS
        g = lax.rem(i, PAIRS)
        rows = pl.ds(pl.multiple_of(u * BLK, BLK), BLK)
        for e in range(2):
            cols = pl.ds(pl.multiple_of((2 * g + e) * DH, DH), DH)
            qt[i, :, e * BLK:(e + 1) * BLK] = q_ref[rows, cols].T
            dot_t[i, :, e * BLK:(e + 1) * BLK] = do_ref[rows, cols].T
        m_run[i] = jnp.full((1, 2 * BLK), 2 * MASKED, F32)
        acc[i] = jnp.zeros((DH + 16, 2 * BLK), F32)
        dqt[i] = jnp.zeros((DH, 2 * BLK), F32)
        return carry

    lax.fori_loop(0, 2 * PAIRS, transpose_pair, 0)
    key_at = lax.broadcasted_iota(jnp.int32, (BLK, 2 * BLK), 0)
    query_at = lax.rem(lax.broadcasted_iota(jnp.int32, (BLK, 2 * BLK), 1), BLK)
    tri[...] = jnp.where(key_at > query_at, MASKED, 0.0)
    dk_acc[...] = jnp.zeros_like(dk_acc)
    dv_acc[...] = jnp.zeros_like(dv_acc)

    starts = []
    for u in range(2):
        end = jnp.int32(0)
        first = jnp.int32(0)
        for d in range(16):
            end = end + len_ref[d]
            first = jnp.where(end <= 2 * c + u, end, first)
        starts.append(first)

    for copy in heads_in:
        copy.wait()

    ctx_in = []
    for o in range(1, 5):
        part = kv.at[0] if o < 4 else kv.at[0, pl.ds(n_head // 2, n_head // 2)]
        there = kv.at[o] if o < 4 else kv.at[4, pl.ds(n_head // 2, n_head // 2)]
        copy = pltpu.make_async_remote_copy(
            src_ref=part, dst_ref=there,
            send_sem=c_send.at[o - 1], recv_sem=c_recv.at[o - 1],
            device_id=after(o), device_id_type=MESH)
        copy.start()
        ctx_in.append(copy)

    def prepare(t):
        if t < 4:
            key = kv[t, :, 0].reshape(2 * BLK, DH)
            val = kv[t, :, 1].reshape(2 * BLK, DH)
        else:
            half = n_head // 2
            key = jnp.concatenate((kv[4, half:, 0].reshape(BLK, DH), kv[0, :half, 0].reshape(BLK, DH)), 0)
            val = jnp.concatenate((kv[4, half:, 1].reshape(BLK, DH), kv[0, :half, 1].reshape(BLK, DH)), 0)
        kk[t] = key
        vv[t] = val
        kt[t] = key.T
        vte[t, :DH] = val.T
        vte[t, DH:] = jnp.ones((16, 2 * BLK), BF)

    def place(u, t):
        return t if u == 1 else t - 1

    def forward(u, t):
        first_unit = 2 * c - 2 * t if t < 4 else 2 * c - 7
        bias0 = jnp.where(first_unit >= starts[u], 0.0, MASKED).astype(F32)
        bias1 = jnp.where(first_unit + 1 >= starts[u], 0.0, MASKED).astype(F32)
        slot = place(u, t)

        def one(g):
            i = u * PAIRS + g
            scores = dot(kk[t], qt[i])
            dp_all[slot, i] = dot(vv[t], dot_t[i])
            low = scores[:BLK] + bias0
            high = scores[BLK:] + (tri[...] if t in (0, 4) else bias1)
            old = m_run[i]
            new = jnp.maximum(old, jnp.max(jnp.maximum(low, high), axis=0, keepdims=True))
            p_low = jnp.exp2((low - new) * C2).astype(BF)
            p_high = jnp.exp2((high - new) * C2).astype(BF)
            weights = jnp.concatenate((p_low, p_high), 0)
            p_all[slot, i] = weights
            m_tile[slot, i] = new
            m_run[i] = new
            acc[i] = acc[i] * jnp.exp2((old - new) * C2) + dot(vte[t], weights)

        def body(step, carry):
            one(2 * step)
            one(2 * step + 1)
            return carry

        lax.fori_loop(0, PAIRS // 2, body, 0)

    prepare(0)
    forward(1, 0)
    for o in range(1, 4):
        ctx_in[o - 1].wait_recv()
        prepare(o)
        forward(0, o)
        forward(1, o)
    ctx_in[3].wait_recv()
    prepare(4)
    forward(0, 4)

    def finish(i, carry):
        u = i // PAIRS
        g = lax.rem(i, PAIRS)
        rows = pl.ds(pl.multiple_of(u * BLK, BLK), BLK)
        total = acc[i, DH:DH + 1]
        inverse = 1.0 / total
        low = (acc[i, :DH] * inverse).astype(BF)
        delta = jnp.sum(low.astype(F32) * dot_t[i].astype(F32), axis=0, keepdims=True)
        acc[i, DH:DH + 1] = inverse
        acc[i, DH + 8:DH + 9] = delta
        for e in range(2):
            cols = pl.ds(pl.multiple_of((2 * g + e) * DH, DH), DH)
            o_out[rows, cols] = low[:, e * BLK:(e + 1) * BLK].T
        return carry

    lax.fori_loop(0, 2 * PAIRS, finish, 0)
    o_copy = pltpu.make_async_copy(o_out, o_hbm, out_sem.at[0])
    o_copy.start()

    def backward(u, t):
        slot = place(u, t)

        def one(g):
            i = u * PAIRS + g
            rows = pl.ds(u * BLK, BLK)
            first = pl.ds(pl.multiple_of(2 * g * DH, DH), DH)
            second = pl.ds(pl.multiple_of((2 * g + 1) * DH, DH), DH)
            queries = jnp.concatenate((q_ref[rows, first], q_ref[rows, second]), 0)
            cotangents = jnp.concatenate((do_ref[rows, first], do_ref[rows, second]), 0)
            factor = jnp.exp2((m_tile[slot, i] - m_run[i]) * C2) * acc[i, DH:DH + 1]
            weights = p_all[slot, i].astype(F32) * factor
            ds = (weights * (dp_all[slot, i] - acc[i, DH + 8:DH + 9])).astype(BF)
            dqt[i] += dot(kt[t], ds)
            return dot(ds, queries), dot(weights.astype(BF), cotangents)

        def body(step, carry):
            dk0, dv0 = one(2 * step)
            dk1, dv1 = one(2 * step + 1)
            dk_acc[t] += dk0 + dk1
            dv_acc[t] += dv0 + dv1
            return carry

        lax.fori_loop(0, PAIRS // 2, body, 0)

    half = n_head // 2
    grads_out = []

    def send(o):
        if o < 4:
            gsend[o, :, 0] = (dk_acc[o] * SCALE).astype(BF).reshape(n_head, 32, DH)
            gsend[o, :, 1] = dv_acc[o].astype(BF).reshape(n_head, 32, DH)
            part, there = gsend.at[o], grecv.at[o]
        else:
            gsend[4, half:, 0] = (dk_acc[4, :BLK] * SCALE).astype(BF).reshape(half, 32, DH)
            gsend[4, half:, 1] = dv_acc[4, :BLK].astype(BF).reshape(half, 32, DH)
            part, there = gsend.at[4, pl.ds(half, half)], grecv.at[4, pl.ds(half, half)]
        copy = pltpu.make_async_remote_copy(
            src_ref=part, dst_ref=there,
            send_sem=g_send.at[o - 1], recv_sem=g_recv.at[o - 1],
            device_id=before(o), device_id_type=MESH)
        copy.start()
        grads_out.append(copy)

    backward(0, 4)
    send(4)
    for o in range(3, 0, -1):
        backward(0, o)
        backward(1, o)
        send(o)
    backward(1, 0)

    def finish_query(i, carry):
        u = i // PAIRS
        g = lax.rem(i, PAIRS)
        rows = pl.ds(pl.multiple_of(u * BLK, BLK), BLK)
        low = (dqt[i] * SCALE).astype(BF)
        for e in range(2):
            cols = pl.ds(pl.multiple_of((2 * g + e) * DH, DH), DH)
            dq_out[rows, cols] = low[:, e * BLK:(e + 1) * BLK].T
        return carry

    lax.fori_loop(0, 2 * PAIRS, finish_query, 0)
    dq_copy = pltpu.make_async_copy(dq_out, dq_hbm, out_sem.at[1])
    dq_copy.start()

    for copy in grads_out:
        copy.wait_recv()
    dk_low = dk_acc[0, :BLK] + dk_acc[4, BLK:]
    dv_low = dv_acc[0, :BLK] + dv_acc[4, BLK:]
    for n, (low, high, scale) in enumerate(
        ((dk_low, dk_acc[0, BLK:], SCALE), (dv_low, dv_acc[0, BLK:], 1.0))):
        low = (low * scale).reshape(half, 32, DH)
        high = (high * scale).reshape(half, 32, DH)
        for o in range(1, 4):
            low = low + grecv[o, :half, n].astype(F32)
            high = high + grecv[o, half:, n].astype(F32)
        high = high + grecv[4, half:, n].astype(F32)
        gown[:half, n] = low.astype(BF)
        gown[half:, n] = high.astype(BF)

    gfin[h] = gown[h]
    heads_out = []
    for j in range(1, n_head):
        copy = pltpu.make_async_remote_copy(
            src_ref=gown.at[lax.rem(h + j, n_head)], dst_ref=gfin.at[h],
            send_sem=b_send.at[j - 1], recv_sem=b_recv.at[j - 1],
            device_id=peer(j), device_id_type=MESH)
        copy.start()
        heads_out.append(copy)
    for copy in ctx_in:
        copy.wait_send()
    for copy in grads_out:
        copy.wait_send()
    for copy in heads_out:
        copy.wait()
    for j in range(n_head):
        dk_ref[:, j * DH:(j + 1) * DH] = gfin[j, 0]
        dv_ref[:, j * DH:(j + 1) * DH] = gfin[j, 1]
    o_copy.wait()
    dq_copy.wait()


def local(query, keys, values, d_out, lengths):
    n_ctx = lax.axis_size("ctx")
    n_head = lax.axis_size("head")
    pairs = 2 * PAIRS
    hbm = pl.BlockSpec(memory_space=pl.ANY)
    vmem = pl.BlockSpec(memory_space=pltpu.VMEM)
    wide = (2 * BLK, GROUP * DH)
    dma = pltpu.SemaphoreType.DMA
    return pl.pallas_call(
        functools.partial(kernel, n_ctx, n_head),
        name="attention",
        out_shape=(
            jax.ShapeDtypeStruct(query.shape, BF),
            jax.ShapeDtypeStruct(query.shape, BF),
            jax.ShapeDtypeStruct(keys.shape, BF),
            jax.ShapeDtypeStruct(keys.shape, BF),
        ),
        in_specs=[pl.BlockSpec(memory_space=pltpu.SMEM), hbm, hbm, hbm, hbm],
        out_specs=(hbm, hbm, vmem, vmem),
        scratch_shapes=[
            pltpu.VMEM(wide, BF),
            pltpu.VMEM(wide, BF),
            pltpu.VMEM(keys.shape, BF),
            pltpu.VMEM(keys.shape, BF),
            pltpu.VMEM((pairs, DH, 2 * BLK), BF),
            pltpu.VMEM((pairs, DH, 2 * BLK), BF),
            pltpu.VMEM((5, n_head, 2, 32, DH), BF),
            pltpu.VMEM((5, 2 * BLK, DH), BF),
            pltpu.VMEM((5, 2 * BLK, DH), BF),
            pltpu.VMEM((5, DH, 2 * BLK), BF),
            pltpu.VMEM((5, DH + 16, 2 * BLK), BF),
            pltpu.VMEM((BLK, 2 * BLK), F32),
            pltpu.VMEM((pairs, 1, 2 * BLK), F32),
            pltpu.VMEM((4, pairs, 1, 2 * BLK), F32),
            pltpu.VMEM((pairs, DH + 16, 2 * BLK), F32),
            pltpu.VMEM((4, pairs, 2 * BLK, 2 * BLK), BF),
            pltpu.VMEM((4, pairs, 2 * BLK, 2 * BLK), F32),
            pltpu.VMEM((pairs, DH, 2 * BLK), F32),
            pltpu.VMEM((5, 2 * BLK, DH), F32),
            pltpu.VMEM((5, 2 * BLK, DH), F32),
            pltpu.VMEM(wide, BF),
            pltpu.VMEM(wide, BF),
            pltpu.VMEM((5, n_head, 2, 32, DH), BF),
            pltpu.VMEM((5, n_head, 2, 32, DH), BF),
            pltpu.VMEM((n_head, 2, 32, DH), BF),
            pltpu.VMEM((n_head, 2, 32, DH), BF),
            pltpu.VMEM((n_head, 2, 32, DH), BF),
            dma((4,)), dma((2,)),
            dma((7,)), dma((7,)), dma((4,)), dma((4,)),
            dma((4,)), dma((4,)), dma((7,)), dma((7,)),
        ],
        compiler_params=pltpu.CompilerParams(
            collective_id=0, has_side_effects=True, vmem_limit_bytes=56 * 2**20
        ),
        cost_estimate=pl.CostEstimate(flops=6500000000, bytes_accessed=5 * 2**20, transcendentals=4500000),
    )(lengths, query, keys, values, d_out)


def solution(mesh):
    in_specs = (
        P("ctx", "head"),
        P(("ctx", "head"), None),
        P(("ctx", "head"), None),
        P("ctx", "head"),
        P(),
    )
    out_specs = (
        P("ctx", "head"),
        P("ctx", "head"),
        P(("ctx", "head"), None),
        P(("ctx", "head"), None),
    )
    return jax.shard_map(local, mesh=mesh, in_specs=in_specs, out_specs=out_specs, check_vma=False)
```

time: 173 us -> 68.5 us (0.40)
  the two profiles are of different devices: /device:TPU:38 before, /device:TPU:1 now
where the time goes in v1:
time: 68.5 us; the launch traced here: 68.3 us
  Pallas kernels  62.8 us (92%)
  local copies, waits for them, and re-layouts  4.86 us (7%)
    pallas_call x1, Pallas kernels, local(): pl.pallas_call(functools.partial(kernel, n_ctx, n_head), name='attention'...  62.8 us
    unnamed x10, local copies, waits for them, and re-layouts  4.86 us

profile of v1, /device:TPU:1, one launch (start us, length us, event | category | flops | bytes accessed | tf_op | source)
XLA Modules:
  0.0 68.3 jit_solution(132790658607739280)
XLA Ops:
  0.6 62.8 %attention.1 = (bf16[256,2048]{1,0:T(8,128)(2,1)}, bf16[256,2048]{1,0:T(8,128)(2,1)}, bf16[32,1024]{1,0:T(8,128)(2,1)}, bf16[32,1024]{1,0:T(8,128)(2,1)}) custom-call(s32[16]{0:T(128)} %len_ref.1, bf16[256,2048]{1,0:T(8,128)(2,1)} %q_hbm.1, bf16[32,1024]{1,0:T(8,128)(2,1)} %k_hbm.1, bf16[32,1024]{1,0:T(8,128)(2,1)} %v_hbm.1, bf16[256,2048]{1,0:T(8,128)(2,1)} %do_hbm.1), custom_call_target="tpu_custom_call" | custom-call | flops 6499999744 | bytes 5242880 | tf_op jit(solution)/shard_map/attention/pallas_call | solution.py:316
  63.4 0.0 copy-start
  63.4 2.4 %copy.13 = bf16[256,2048]{1,0:T(8,128)(2,1)} copy(bf16[256,2048]{1,0:T(8,128)(2,1)} %get-tuple-element.8) | data formatting | bytes 2097152
  65.8 0.0 copy-done
  65.8 0.0 copy-start.2
  65.8 1.0 %copy.14 = bf16[256,2048]{1,0:T(8,128)(2,1)} copy(bf16[256,2048]{1,0:T(8,128)(2,1)S(1)} %copy-done) | data formatting | bytes 2097152
  66.8 0.0 copy-done.2
  66.8 0.0 copy-start.1
  66.8 0.6 copy.15
  67.4 0.2 copy-done.1
  67.7 0.6 copy.16
Async XLA Ops:
  63.4 2.4 %copy-start = (bf16[256,2048]{1,0:T(8,128)(2,1)S(1)}, bf16[256,2048]{1,0:T(8,128)(2,1)}, u32[]{:S(2)}) copy-start(bf16[256,2048]{1,0:T(8,128)(2,1)} %get-tuple-element.9) | copy-start | bytes 3145732
  65.8 1.0 %copy-start.2 = (bf16[32,1024]{1,0:T(8,128)(2,1)S(1)}, bf16[32,1024]{1,0:T(8,128)(2,1)}, u32[]{:S(2)}) copy-start(bf16[32,1024]{1,0:T(8,128)(2,1)} %get-tuple-element.10) | copy-start | bytes 196612
  66.8 0.9 %copy-start.1 = (bf16[32,1024]{1,0:T(8,128)(2,1)S(1)}, bf16[32,1024]{1,0:T(8,128)(2,1)}, u32[]{:S(2)}) copy-start(bf16[32,1024]{1,0:T(8,128)(2,1)} %get-tuple-element.11) | copy-start | bytes 196612

commit v2 on v1

--- a/solution.py
+++ b/solution.py
@@ -26,20 +26,35 @@
     return lax.dot_general(a, b, (((1,), (0,)), ((), ())), preferred_element_type=F32)
 
 
+def write_out(*refs):
+    sem = refs[8]
+    copies = [pltpu.make_async_copy(refs[n], refs[4 + n], sem.at[n]) for n in range(4)]
+    for copy in copies:
+        copy.start()
+    for copy in copies:
+        copy.wait()
+
+
 def kernel(
     n_ctx, n_head,
     len_ref, q_hbm, k_hbm, v_hbm, do_hbm,
-    o_hbm, dq_hbm, dk_ref, dv_ref,
+    o_out, dq_out, dk_ref, dv_ref,
     q_ref, do_ref, k_ref, v_ref, qt, dot_t, kv, kk, vv, kt, vte, tri,
     m_run, m_tile, acc, p_all, dp_all, dqt, dk_acc, dv_acc,
-    o_out, dq_out, gsend, grecv, gown, gfin, stage,
-    load_sem, out_sem, a_send, a_recv, c_send, c_recv, g_send, g_recv, b_send, b_recv,
+    gsend, grecv, gown, gfin, stage,
+    load_sem, a_send, a_recv, c_send, c_recv, g_send, g_recv, b_send, b_recv,
 ):
     c = lax.axis_index("ctx")
     h = lax.axis_index("head")
 
+    chips = n_head // 2
+    order = [(0, 1)] + [(d, e) for d in (1, 3, 2) for e in (0, 1)]
+
+    def head_at(d, e):
+        return 2 * lax.rem(h // 2 + d, chips) + lax.rem(h + e, 2)
+
     def peer(j):
-        return (c, lax.rem(h + j, n_head))
+        return (c, head_at(*order[j - 1]))
 
     def after(o):
         return (lax.rem(c + o, n_ctx), h)
@@ -71,14 +86,15 @@
     kv[0, h] = stage[h]
     pl.semaphore_wait(barrier, n_head - 1 + 8)
 
-    heads_in = []
-    for j in range(1, n_head):
+    heads_in = {}
+    for n, (d, e) in enumerate(order):
+        target = head_at(d, e)
         copy = pltpu.make_async_remote_copy(
-            src_ref=stage.at[lax.rem(h + j, n_head)], dst_ref=kv.at[0, h],
-            send_sem=a_send.at[j - 1], recv_sem=a_recv.at[j - 1],
-            device_id=peer(j), device_id_type=MESH)
-        copy.start()
-        heads_in.append(copy)
+            src_ref=stage.at[target], dst_ref=kv.at[0, h],
+            send_sem=a_send.at[n], recv_sem=a_recv.at[n],
+            device_id=(c, target), device_id_type=MESH)
+        copy.start()
+        heads_in[d, e] = copy
 
     loads[2].wait()
     loads[3].wait()
@@ -96,7 +112,7 @@
         dqt[i] = jnp.zeros((DH, 2 * BLK), F32)
         return carry
 
-    lax.fori_loop(0, 2 * PAIRS, transpose_pair, 0)
+    lax.fori_loop(0, 2 * PAIRS, transpose_pair, 0, unroll=2)
     key_at = lax.broadcasted_iota(jnp.int32, (BLK, 2 * BLK), 0)
     query_at = lax.rem(lax.broadcasted_iota(jnp.int32, (BLK, 2 * BLK), 1), BLK)
     tri[...] = jnp.where(key_at > query_at, MASKED, 0.0)
@@ -112,19 +128,31 @@
             first = jnp.where(end <= 2 * c + u, end, first)
         starts.append(first)
 
-    for copy in heads_in:
-        copy.wait()
-
-    ctx_in = []
-    for o in range(1, 5):
-        part = kv.at[0] if o < 4 else kv.at[0, pl.ds(n_head // 2, n_head // 2)]
-        there = kv.at[o] if o < 4 else kv.at[4, pl.ds(n_head // 2, n_head // 2)]
-        copy = pltpu.make_async_remote_copy(
-            src_ref=part, dst_ref=there,
-            send_sem=c_send.at[o - 1], recv_sem=c_recv.at[o - 1],
+    def onward(d, o):
+        first = 2 * lax.rem(h // 2 + chips - d, chips)
+        return first >= n_head // 2, pltpu.make_async_remote_copy(
+            src_ref=kv.at[0, pl.ds(first, 2)], dst_ref=kv.at[o, pl.ds(first, 2)],
+            send_sem=c_send.at[o - 1, d], recv_sem=c_recv.at[o - 1, d],
             device_id=after(o), device_id_type=MESH)
-        copy.start()
-        ctx_in.append(copy)
+
+    def each_part(o, act):
+        for d in range(chips):
+            late, copy = onward(d, o)
+            if o < 4:
+                act(copy)
+            else:
+                pl.when(late)(functools.partial(act, copy))
+
+    for d in (0, 1, 3, 2):
+        for e in (0, 1):
+            if (d, e) in heads_in:
+                heads_in[d, e].wait_recv()
+        for o in range(1, 5):
+            late, copy = onward(d, o)
+            if o < 4:
+                copy.start()
+            else:
+                pl.when(late)(copy.start)
 
     def prepare(t):
         if t < 4:
@@ -165,42 +193,25 @@
             m_run[i] = new
             acc[i] = acc[i] * jnp.exp2((old - new) * C2) + dot(vte[t], weights)
 
-        def body(step, carry):
-            one(2 * step)
-            one(2 * step + 1)
-            return carry
-
-        lax.fori_loop(0, PAIRS // 2, body, 0)
+        for g in range(PAIRS):
+            one(g)
 
     prepare(0)
     forward(1, 0)
     for o in range(1, 4):
-        ctx_in[o - 1].wait_recv()
+        each_part(o, lambda copy: copy.wait_recv())
         prepare(o)
         forward(0, o)
         forward(1, o)
-    ctx_in[3].wait_recv()
+    each_part(4, lambda copy: copy.wait_recv())
     prepare(4)
     forward(0, 4)
 
-    def finish(i, carry):
-        u = i // PAIRS
-        g = lax.rem(i, PAIRS)
-        rows = pl.ds(pl.multiple_of(u * BLK, BLK), BLK)
-        total = acc[i, DH:DH + 1]
-        inverse = 1.0 / total
+    for i in range(2 * PAIRS):
+        inverse = 1.0 / acc[i, DH:DH + 1]
         low = (acc[i, :DH] * inverse).astype(BF)
-        delta = jnp.sum(low.astype(F32) * dot_t[i].astype(F32), axis=0, keepdims=True)
         acc[i, DH:DH + 1] = inverse
-        acc[i, DH + 8:DH + 9] = delta
-        for e in range(2):
-            cols = pl.ds(pl.multiple_of((2 * g + e) * DH, DH), DH)
-            o_out[rows, cols] = low[:, e * BLK:(e + 1) * BLK].T
-        return carry
-
-    lax.fori_loop(0, 2 * PAIRS, finish, 0)
-    o_copy = pltpu.make_async_copy(o_out, o_hbm, out_sem.at[0])
-    o_copy.start()
+        acc[i, DH + 8:DH + 9] = jnp.sum(low.astype(F32) * dot_t[i].astype(F32), axis=0, keepdims=True)
 
     def backward(u, t):
         slot = place(u, t)
@@ -208,8 +219,8 @@
         def one(g):
             i = u * PAIRS + g
             rows = pl.ds(u * BLK, BLK)
-            first = pl.ds(pl.multiple_of(2 * g * DH, DH), DH)
-            second = pl.ds(pl.multiple_of((2 * g + 1) * DH, DH), DH)
+            first = pl.ds(2 * g * DH, DH)
+            second = pl.ds((2 * g + 1) * DH, DH)
             queries = jnp.concatenate((q_ref[rows, first], q_ref[rows, second]), 0)
             cotangents = jnp.concatenate((do_ref[rows, first], do_ref[rows, second]), 0)
             factor = jnp.exp2((m_tile[slot, i] - m_run[i]) * C2) * acc[i, DH:DH + 1]
@@ -218,14 +229,9 @@
             dqt[i] += dot(kt[t], ds)
             return dot(ds, queries), dot(weights.astype(BF), cotangents)
 
-        def body(step, carry):
-            dk0, dv0 = one(2 * step)
-            dk1, dv1 = one(2 * step + 1)
-            dk_acc[t] += dk0 + dk1
-            dv_acc[t] += dv0 + dv1
-            return carry
-
-        lax.fori_loop(0, PAIRS // 2, body, 0)
+        sums = [one(g) for g in range(PAIRS)]
+        dk_acc[t] += sum(pair[0] for pair in sums)
+        dv_acc[t] += sum(pair[1] for pair in sums)
 
     half = n_head // 2
     grads_out = []
@@ -254,19 +260,19 @@
         send(o)
     backward(1, 0)
 
-    def finish_query(i, carry):
+    def finish(i, carry):
         u = i // PAIRS
         g = lax.rem(i, PAIRS)
         rows = pl.ds(pl.multiple_of(u * BLK, BLK), BLK)
         low = (dqt[i] * SCALE).astype(BF)
+        out = (acc[i, :DH] * acc[i, DH:DH + 1]).astype(BF)
         for e in range(2):
             cols = pl.ds(pl.multiple_of((2 * g + e) * DH, DH), DH)
             dq_out[rows, cols] = low[:, e * BLK:(e + 1) * BLK].T
+            o_out[rows, cols] = out[:, e * BLK:(e + 1) * BLK].T
         return carry
 
-    lax.fori_loop(0, 2 * PAIRS, finish_query, 0)
-    dq_copy = pltpu.make_async_copy(dq_out, dq_hbm, out_sem.at[1])
-    dq_copy.start()
+    lax.fori_loop(0, 2 * PAIRS, finish, 0, unroll=2)
 
     for copy in grads_out:
         copy.wait_recv()
@@ -285,15 +291,18 @@
 
     gfin[h] = gown[h]
     heads_out = []
-    for j in range(1, n_head):
+    for n, (d, e) in enumerate(order):
+        target = head_at(d, e)
         copy = pltpu.make_async_remote_copy(
-            src_ref=gown.at[lax.rem(h + j, n_head)], dst_ref=gfin.at[h],
-            send_sem=b_send.at[j - 1], recv_sem=b_recv.at[j - 1],
-            device_id=peer(j), device_id_type=MESH)
+            src_ref=gown.at[target], dst_ref=gfin.at[h],
+            send_sem=b_send.at[n], recv_sem=b_recv.at[n],
+            device_id=(c, target), device_id_type=MESH)
         copy.start()
         heads_out.append(copy)
-    for copy in ctx_in:
+    for copy in heads_in.values():
         copy.wait_send()
+    for o in range(1, 5):
+        each_part(o, lambda copy: copy.wait_send())
     for copy in grads_out:
         copy.wait_send()
     for copy in heads_out:
@@ -301,8 +310,6 @@
     for j in range(n_head):
         dk_ref[:, j * DH:(j + 1) * DH] = gfin[j, 0]
         dv_ref[:, j * DH:(j + 1) * DH] = gfin[j, 1]
-    o_copy.wait()
-    dq_copy.wait()
 
 
 def local(query, keys, values, d_out, lengths):
@@ -313,17 +320,17 @@
     vmem = pl.BlockSpec(memory_space=pltpu.VMEM)
     wide = (2 * BLK, GROUP * DH)
     dma = pltpu.SemaphoreType.DMA
-    return pl.pallas_call(
+    held = pl.pallas_call(
         functools.partial(kernel, n_ctx, n_head),
         name="attention",
         out_shape=(
-            jax.ShapeDtypeStruct(query.shape, BF),
-            jax.ShapeDtypeStruct(query.shape, BF),
-            jax.ShapeDtypeStruct(keys.shape, BF),
-            jax.ShapeDtypeStruct(keys.shape, BF),
+            pltpu.VMEM(query.shape, BF),
+            pltpu.VMEM(query.shape, BF),
+            pltpu.VMEM(keys.shape, BF),
+            pltpu.VMEM(keys.shape, BF),
         ),
         in_specs=[pl.BlockSpec(memory_space=pltpu.SMEM), hbm, hbm, hbm, hbm],
-        out_specs=(hbm, hbm, vmem, vmem),
+        out_specs=(vmem, vmem, vmem, vmem),
         scratch_shapes=[
             pltpu.VMEM(wide, BF),
             pltpu.VMEM(wide, BF),
@@ -345,15 +352,13 @@
             pltpu.VMEM((pairs, DH, 2 * BLK), F32),
             pltpu.VMEM((5, 2 * BLK, DH), F32),
             pltpu.VMEM((5, 2 * BLK, DH), F32),
-            pltpu.VMEM(wide, BF),
-            pltpu.VMEM(wide, BF),
             pltpu.VMEM((5, n_head, 2, 32, DH), BF),
             pltpu.VMEM((5, n_head, 2, 32, DH), BF),
             pltpu.VMEM((n_head, 2, 32, DH), BF),
             pltpu.VMEM((n_head, 2, 32, DH), BF),
             pltpu.VMEM((n_head, 2, 32, DH), BF),
-            dma((4,)), dma((2,)),
-            dma((7,)), dma((7,)), dma((4,)), dma((4,)),
+            dma((4,)),
+            dma((7,)), dma((7,)), dma((4, 4)), dma((4, 4)),
             dma((4,)), dma((4,)), dma((7,)), dma((7,)),
         ],
         compiler_params=pltpu.CompilerParams(
@@ -361,6 +366,14 @@
         ),
         cost_estimate=pl.CostEstimate(flops=6500000000, bytes_accessed=5 * 2**20, transcendentals=4500000),
     )(lengths, query, keys, values, d_out)
+    return pl.pallas_call(
+        write_out,
+        name="write_out",
+        out_shape=tuple(jax.ShapeDtypeStruct(x.shape, BF) for x in (query, query, keys, keys)),
+        in_specs=[vmem] * 4,
+        out_specs=(hbm,) * 4,
+        scratch_shapes=[dma((4,))],
+    )(*(pltpu.with_memory_space_constraint(x, pltpu.VMEM) for x in held))
 
 
 def solution(mesh):

time: 68.5 us -> 53.2 us (0.78); the launches traced: 68.3 us -> 52.2 us
  Pallas kernels: 62.8 us -> 51.4 us
  local copies, waits for them, and re-layouts: 4.86 us -> 0 us
    pallas_call x1, Pallas kernels: 62.8 us -> 50 us  [local(): pl.pallas_call(functools.partial(kernel, n_ctx, n_head), name='attention'...]
    unnamed x10 -> x0, local copies, waits for them, and re-layouts: 4.86 us -> none
    pallas_call x0 -> x1, Pallas kernels: none -> 1.38 us  [local(): pl.pallas_call(write_out, name='write_out', out_shape=tuple((jax.ShapeDty...]
where the time goes in v2:
time: 53.2 us; the launch traced here: 52.2 us
  Pallas kernels  51.4 us (97%)
  between operations  0.8 us (2%)
    pallas_call x1, Pallas kernels, local(): pl.pallas_call(functools.partial(kernel, n_ctx, n_head), name='attention'...  50 us
    pallas_call x1, Pallas kernels, local(): pl.pallas_call(write_out, name='write_out', out_shape=tuple((jax.ShapeDty...  1.38 us

profile of v2, /device:TPU:1, one launch (start us, length us, event | category | flops | bytes accessed | tf_op | source)
XLA Modules:
  0.0 52.2 jit_solution(5086996960287249277)
XLA Ops:
  0.6 50.0 %attention.1 = (bf16[256,2048]{1,0:T(8,128)(2,1)S(1)}, bf16[256,2048]{1,0:T(8,128)(2,1)S(1)}, bf16[32,1024]{1,0:T(8,128)(2,1)S(1)}, bf16[32,1024]{1,0:T(8,128)(2,1)S(1)}) custom-call(s32[16]{0:T(128)} %len_ref.1, bf16[256,2048]{1,0:T(8,128)(2,1)} %q_hbm.1, bf16[32,1024]{1,0:T(8,128)(2,1)} %k_hbm.1, bf16[32,1024]{1,0:T(8,128)(2,1)} %v_hbm.1, ...), custom_call_target="tpu_custom_call" | custom-call | flops 6499999744 | bytes 5242880 | tf_op jit(solution)/shard_map/attention/pallas_call | solution.py:323
  50.7 1.4 %write_out.1 = (bf16[256,2048]{1,0:T(8,128)(2,1)}, bf16[256,2048]{1,0:T(8,128)(2,1)}, bf16[32,1024]{1,0:T(8,128)(2,1)}, bf16[32,1024]{1,0:T(8,128)(2,1)}) custom-call(bf16[256,2048]{1,0:T(8,128)(2,1)S(1)} %get-tuple-element.8.refs_0_, bf16[256,2048]{1,0:T(8,128)(2,1)S(1)} %get-tuple-element.9.refs_1_, bf16[32,1024]{1,0:T(8,128)(2,1)S(1)} %get-tuple-element.10.refs_2_, ...), custom_call_target="tpu_custom_call" | custom-call | tf_op jit(solution)/shard_map/write_out/pallas_call | solution.py:369

commit v3 on v2

--- a/solution.py
+++ b/solution.py
@@ -40,8 +40,8 @@
     len_ref, q_hbm, k_hbm, v_hbm, do_hbm,
     o_out, dq_out, dk_ref, dv_ref,
     q_ref, do_ref, k_ref, v_ref, qt, dot_t, kv, kk, vv, kt, vte, tri,
-    m_run, m_tile, acc, p_all, dp_all, dqt, dk_acc, dv_acc,
-    gsend, grecv, gown, gfin, stage,
+    m_run, m_tile, acc, p_all, dp_all, s_all, dqt, dk_acc, dv_acc,
+    gsend, grecv, own, gown, gfin, stage,
     load_sem, a_send, a_recv, c_send, c_recv, g_send, g_recv, b_send, b_recv,
 ):
     c = lax.axis_index("ctx")
@@ -61,6 +61,13 @@
 
     def before(o):
         return (lax.rem(c + n_ctx - o, n_ctx), h)
+
+    barrier = pltpu.get_barrier_semaphore()
+    for j in range(1, n_head):
+        pl.semaphore_signal(barrier, inc=1, device_id=peer(j), device_id_type=MESH)
+    for o in range(1, 5):
+        pl.semaphore_signal(barrier, inc=1, device_id=after(o), device_id_type=MESH)
+        pl.semaphore_signal(barrier, inc=1, device_id=before(o), device_id_type=MESH)
 
     loads = [
         pltpu.make_async_copy(k_hbm, k_ref, load_sem.at[0]),
@@ -70,13 +77,6 @@
     ]
     for copy in loads:
         copy.start()
-
-    barrier = pltpu.get_barrier_semaphore()
-    for j in range(1, n_head):
-        pl.semaphore_signal(barrier, inc=1, device_id=peer(j), device_id_type=MESH)
-    for o in range(1, 5):
-        pl.semaphore_signal(barrier, inc=1, device_id=after(o), device_id_type=MESH)
-        pl.semaphore_signal(barrier, inc=1, device_id=before(o), device_id_type=MESH)
 
     loads[0].wait()
     loads[1].wait()
@@ -128,6 +128,8 @@
             first = jnp.where(end <= 2 * c + u, end, first)
         starts.append(first)
 
+    half = n_head // 2
+
     def onward(d, o):
         first = 2 * lax.rem(h // 2 + chips - d, chips)
         return first >= n_head // 2, pltpu.make_async_remote_copy(
@@ -159,7 +161,6 @@
             key = kv[t, :, 0].reshape(2 * BLK, DH)
             val = kv[t, :, 1].reshape(2 * BLK, DH)
         else:
-            half = n_head // 2
             key = jnp.concatenate((kv[4, half:, 0].reshape(BLK, DH), kv[0, :half, 0].reshape(BLK, DH)), 0)
             val = jnp.concatenate((kv[4, half:, 1].reshape(BLK, DH), kv[0, :half, 1].reshape(BLK, DH)), 0)
         kk[t] = key
@@ -177,41 +178,37 @@
         bias1 = jnp.where(first_unit + 1 >= starts[u], 0.0, MASKED).astype(F32)
         slot = place(u, t)
 
-        def one(g):
-            i = u * PAIRS + g
-            scores = dot(kk[t], qt[i])
+        last = tri[...] if t in (0, 4) else bias1
+        span = range(u * PAIRS, (u + 1) * PAIRS)
+        for i in span:
+            s_all[i % PAIRS] = dot(kk[t], qt[i])
             dp_all[slot, i] = dot(vv[t], dot_t[i])
-            low = scores[:BLK] + bias0
-            high = scores[BLK:] + (tri[...] if t in (0, 4) else bias1)
-            old = m_run[i]
-            new = jnp.maximum(old, jnp.max(jnp.maximum(low, high), axis=0, keepdims=True))
-            p_low = jnp.exp2((low - new) * C2).astype(BF)
-            p_high = jnp.exp2((high - new) * C2).astype(BF)
-            weights = jnp.concatenate((p_low, p_high), 0)
-            p_all[slot, i] = weights
-            m_tile[slot, i] = new
+        for i in span:
+            g = i % PAIRS
+            top = jnp.maximum(s_all[g, :BLK] + bias0, s_all[g, BLK:] + last)
+            m_tile[slot, i] = jnp.maximum(m_run[i], jnp.max(top, axis=0, keepdims=True))
+        for i in span:
+            g = i % PAIRS
+            new = m_tile[slot, i]
+            p_all[slot, i, :BLK] = jnp.exp2((s_all[g, :BLK] + bias0 - new) * C2).astype(BF)
+            p_all[slot, i, BLK:] = jnp.exp2((s_all[g, BLK:] + last - new) * C2).astype(BF)
+            acc[i] = acc[i] * jnp.exp2((m_run[i] - new) * C2) + dot(vte[t], p_all[slot, i])
             m_run[i] = new
-            acc[i] = acc[i] * jnp.exp2((old - new) * C2) + dot(vte[t], weights)
-
-        for g in range(PAIRS):
-            one(g)
 
     prepare(0)
     forward(1, 0)
     for o in range(1, 4):
         each_part(o, lambda copy: copy.wait_recv())
         prepare(o)
+        forward(1, o)
         forward(0, o)
-        forward(1, o)
-    each_part(4, lambda copy: copy.wait_recv())
-    prepare(4)
-    forward(0, 4)
-
-    for i in range(2 * PAIRS):
-        inverse = 1.0 / acc[i, DH:DH + 1]
-        low = (acc[i, :DH] * inverse).astype(BF)
-        acc[i, DH:DH + 1] = inverse
-        acc[i, DH + 8:DH + 9] = jnp.sum(low.astype(F32) * dot_t[i].astype(F32), axis=0, keepdims=True)
+
+    def close(u):
+        for i in range(u * PAIRS, (u + 1) * PAIRS):
+            inverse = 1.0 / acc[i, DH:DH + 1]
+            low = (acc[i, :DH] * inverse).astype(BF)
+            acc[i, DH:DH + 1] = inverse
+            acc[i, DH + 8:DH + 9] = jnp.sum(low.astype(F32) * dot_t[i].astype(F32), axis=0, keepdims=True)
 
     def backward(u, t):
         slot = place(u, t)
@@ -233,32 +230,55 @@
         dk_acc[t] += sum(pair[0] for pair in sums)
         dv_acc[t] += sum(pair[1] for pair in sums)
 
-    half = n_head // 2
-    grads_out = []
+    out_order = (2, 1, 3, 0)
+
+    def back(d, o):
+        first = 2 * lax.rem(h // 2 + d, chips)
+        return first, pltpu.make_async_remote_copy(
+            src_ref=gsend.at[o, pl.ds(first, 2)], dst_ref=grecv.at[o, pl.ds(first, 2)],
+            send_sem=g_send.at[o - 1, d], recv_sem=g_recv.at[o - 1, d],
+            device_id=before(o), device_id_type=MESH)
+
+    def each_back(d, o, act):
+        first, copy = back(d, o)
+        if o < 4:
+            act(copy)
+        else:
+            pl.when(first >= half)(functools.partial(act, copy))
 
     def send(o):
         if o < 4:
             gsend[o, :, 0] = (dk_acc[o] * SCALE).astype(BF).reshape(n_head, 32, DH)
             gsend[o, :, 1] = dv_acc[o].astype(BF).reshape(n_head, 32, DH)
-            part, there = gsend.at[o], grecv.at[o]
         else:
             gsend[4, half:, 0] = (dk_acc[4, :BLK] * SCALE).astype(BF).reshape(half, 32, DH)
             gsend[4, half:, 1] = dv_acc[4, :BLK].astype(BF).reshape(half, 32, DH)
-            part, there = gsend.at[4, pl.ds(half, half)], grecv.at[4, pl.ds(half, half)]
-        copy = pltpu.make_async_remote_copy(
-            src_ref=part, dst_ref=there,
-            send_sem=g_send.at[o - 1], recv_sem=g_recv.at[o - 1],
-            device_id=before(o), device_id_type=MESH)
-        copy.start()
-        grads_out.append(copy)
-
+        for d in out_order:
+            each_back(d, o, lambda copy: copy.start())
+
+    grecv[4, :half] = jnp.zeros((half, 2, 32, DH), BF)
+    close(1)
+    each_part(4, lambda copy: copy.wait_recv())
+    prepare(4)
+    forward(0, 4)
+    close(0)
     backward(0, 4)
     send(4)
-    for o in range(3, 0, -1):
-        backward(0, o)
-        backward(1, o)
-        send(o)
+    backward(0, 3)
+    backward(1, 3)
+    send(3)
+    backward(0, 2)
+    backward(1, 2)
+    send(2)
+    backward(0, 1)
+    backward(1, 1)
+    send(1)
     backward(1, 0)
+
+    own[:, 0] = (dk_acc[0] * SCALE).reshape(n_head, 32, DH)
+    own[:, 1] = dv_acc[0].reshape(n_head, 32, DH)
+    own[:half, 0] += (dk_acc[4, BLK:] * SCALE).reshape(half, 32, DH)
+    own[:half, 1] += dv_acc[4, BLK:].reshape(half, 32, DH)
 
     def finish(i, carry):
         u = i // PAIRS
@@ -274,37 +294,35 @@
 
     lax.fori_loop(0, 2 * PAIRS, finish, 0, unroll=2)
 
-    for copy in grads_out:
-        copy.wait_recv()
-    dk_low = dk_acc[0, :BLK] + dk_acc[4, BLK:]
-    dv_low = dv_acc[0, :BLK] + dv_acc[4, BLK:]
-    for n, (low, high, scale) in enumerate(
-        ((dk_low, dk_acc[0, BLK:], SCALE), (dv_low, dv_acc[0, BLK:], 1.0))):
-        low = (low * scale).reshape(half, 32, DH)
-        high = (high * scale).reshape(half, 32, DH)
-        for o in range(1, 4):
-            low = low + grecv[o, :half, n].astype(F32)
-            high = high + grecv[o, half:, n].astype(F32)
-        high = high + grecv[4, half:, n].astype(F32)
-        gown[:half, n] = low.astype(BF)
-        gown[half:, n] = high.astype(BF)
-
+    heads_out = []
+    for d in out_order:
+        for o in range(4, 0, -1):
+            each_back(d, o, lambda copy: copy.wait_recv())
+        first = 2 * lax.rem(h // 2 + d, chips)
+        part = pl.ds(first, 2)
+        total = own[part]
+        for o in range(1, 5):
+            total = total + grecv[o, part].astype(F32)
+        gown[part] = total.astype(BF)
+        for e in (0, 1):
+            if (d, e) == (0, 0):
+                continue
+            n = order.index((d, e))
+            target = head_at(d, e)
+            copy = pltpu.make_async_remote_copy(
+                src_ref=gown.at[target], dst_ref=gfin.at[h],
+                send_sem=b_send.at[n], recv_sem=b_recv.at[n],
+                device_id=(c, target), device_id_type=MESH)
+            copy.start()
+            heads_out.append(copy)
     gfin[h] = gown[h]
-    heads_out = []
-    for n, (d, e) in enumerate(order):
-        target = head_at(d, e)
-        copy = pltpu.make_async_remote_copy(
-            src_ref=gown.at[target], dst_ref=gfin.at[h],
-            send_sem=b_send.at[n], recv_sem=b_recv.at[n],
-            device_id=(c, target), device_id_type=MESH)
-        copy.start()
-        heads_out.append(copy)
     for copy in heads_in.values():
         copy.wait_send()
     for o in range(1, 5):
         each_part(o, lambda copy: copy.wait_send())
-    for copy in grads_out:
-        copy.wait_send()
+    for d in out_order:
+        for o in range(1, 5):
+            each_back(d, o, lambda copy: copy.wait_send())
     for copy in heads_out:
         copy.wait()
     for j in range(n_head):
@@ -349,17 +367,19 @@
             pltpu.VMEM((pairs, DH + 16, 2 * BLK), F32),
             pltpu.VMEM((4, pairs, 2 * BLK, 2 * BLK), BF),
             pltpu.VMEM((4, pairs, 2 * BLK, 2 * BLK), F32),
+            pltpu.VMEM((PAIRS, 2 * BLK, 2 * BLK), F32),
             pltpu.VMEM((pairs, DH, 2 * BLK), F32),
             pltpu.VMEM((5, 2 * BLK, DH), F32),
             pltpu.VMEM((5, 2 * BLK, DH), F32),
             pltpu.VMEM((5, n_head, 2, 32, DH), BF),
             pltpu.VMEM((5, n_head, 2, 32, DH), BF),
+            pltpu.VMEM((n_head, 2, 32, DH), F32),
             pltpu.VMEM((n_head, 2, 32, DH), BF),
             pltpu.VMEM((n_head, 2, 32, DH), BF),
             pltpu.VMEM((n_head, 2, 32, DH), BF),
             dma((4,)),
             dma((7,)), dma((7,)), dma((4, 4)), dma((4, 4)),
-            dma((4,)), dma((4,)), dma((7,)), dma((7,)),
+            dma((4, 4)), dma((4, 4)), dma((7,)), dma((7,)),
         ],
         compiler_params=pltpu.CompilerParams(
             collective_id=0, has_side_effects=True, vmem_limit_bytes=56 * 2**20

time: 53.2 us -> 50.8 us (0.955); the launches traced: 52.2 us -> 50.6 us
  Pallas kernels: 51.4 us -> 49.8 us
    pallas_call x1, Pallas kernels: 50 us -> 48.5 us  [local(): pl.pallas_call(functools.partial(kernel, n_ctx, n_head), name='attention'...]
where the time goes in v3:
time: 50.8 us; the launch traced here: 50.6 us
  Pallas kernels  49.8 us (98%)
  between operations  0.8 us (2%)
    pallas_call x1, Pallas kernels, local(): pl.pallas_call(functools.partial(kernel, n_ctx, n_head), name='attention'...  48.5 us
    pallas_call x1, Pallas kernels, local(): pl.pallas_call(write_out, name='write_out', out_shape=tuple((jax.ShapeDty...  1.38 us

profile of v3, /device:TPU:1, one launch (start us, length us, event | category | flops | bytes accessed | tf_op | source)
XLA Modules:
  0.0 50.6 jit_solution(12376256857474575663)
XLA Ops:
  0.6 48.5 %attention.1 = (bf16[256,2048]{1,0:T(8,128)(2,1)S(1)}, bf16[256,2048]{1,0:T(8,128)(2,1)S(1)}, bf16[32,1024]{1,0:T(8,128)(2,1)S(1)}, bf16[32,1024]{1,0:T(8,128)(2,1)S(1)}) custom-call(s32[16]{0:T(128)} %len_ref.1, bf16[256,2048]{1,0:T(8,128)(2,1)} %q_hbm.1, bf16[32,1024]{1,0:T(8,128)(2,1)} %k_hbm.1, bf16[32,1024]{1,0:T(8,128)(2,1)} %v_hbm.1, ...), custom_call_target="tpu_custom_call" | custom-call | flops 6499999744 | bytes 5242880 | tf_op jit(solution)/shard_map/attention/pallas_call | solution.py:341
  49.1 1.4 %write_out.1 = (bf16[256,2048]{1,0:T(8,128)(2,1)}, bf16[256,2048]{1,0:T(8,128)(2,1)}, bf16[32,1024]{1,0:T(8,128)(2,1)}, bf16[32,1024]{1,0:T(8,128)(2,1)}) custom-call(bf16[256,2048]{1,0:T(8,128)(2,1)S(1)} %get-tuple-element.8.refs_0_, bf16[256,2048]{1,0:T(8,128)(2,1)S(1)} %get-tuple-element.9.refs_1_, bf16[32,1024]{1,0:T(8,128)(2,1)S(1)} %get-tuple-element.10.refs_2_, ...), custom_call_target="tpu_custom_call" | custom-call | tf_op jit(solution)/shard_map/write_out/pallas_call | solution.py:389

commit v4 on v3

--- a/solution.py
+++ b/solution.py
@@ -28,7 +28,12 @@
 
 def write_out(*refs):
     sem = refs[8]
-    copies = [pltpu.make_async_copy(refs[n], refs[4 + n], sem.at[n]) for n in range(4)]
+    copies = [pltpu.make_async_copy(refs[n], refs[4 + n], sem.at[n]) for n in (2, 3)]
+    for n in range(2):
+        for part in range(4):
+            rows = pl.ds(part * 64, 64)
+            copies.append(pltpu.make_async_copy(
+                refs[n].at[rows], refs[4 + n].at[rows], sem.at[4 + 4 * n + part]))
     for copy in copies:
         copy.start()
     for copy in copies:
@@ -96,8 +101,32 @@
         copy.start()
         heads_in[d, e] = copy
 
-    loads[2].wait()
-    loads[3].wait()
+    def onward(d, o):
+        first = 2 * lax.rem(h // 2 + chips - d, chips)
+        return first >= n_head // 2, pltpu.make_async_remote_copy(
+            src_ref=kv.at[0, pl.ds(first, 2)], dst_ref=kv.at[o, pl.ds(first, 2)],
+            send_sem=c_send.at[o - 1, d], recv_sem=c_recv.at[o - 1, d],
+            device_id=after(o), device_id_type=MESH)
+
+    def each_part(o, act):
+        for d in range(chips):
+            late, copy = onward(d, o)
+            if o < 4:
+                act(copy)
+            else:
+                pl.when(late)(functools.partial(act, copy))
+
+    def push(d, places):
+        for e in (0, 1):
+            if (d, e) in heads_in and (d, e) not in arrived:
+                heads_in[d, e].wait_recv()
+                arrived.add((d, e))
+        for o in places:
+            last, copy = onward(d, o)
+            if o < 4:
+                copy.start()
+            else:
+                pl.when(last)(copy.start)
 
     def transpose_pair(i, carry):
         u = i // PAIRS
@@ -112,7 +141,18 @@
         dqt[i] = jnp.zeros((DH, 2 * BLK), F32)
         return carry
 
-    lax.fori_loop(0, 2 * PAIRS, transpose_pair, 0, unroll=2)
+    arrived = set()
+    push(0, (1, 2))
+    loads[2].wait()
+    loads[3].wait()
+    lax.fori_loop(PAIRS, 2 * PAIRS, transpose_pair, 0, unroll=2)
+    push(1, (1, 2))
+    push(3, (1, 2))
+    lax.fori_loop(0, PAIRS, transpose_pair, 0, unroll=2)
+    push(2, (1, 2))
+    for o in [3, 4]:
+        for d in (0, 1, 3, 2):
+            push(d, (o,))
     key_at = lax.broadcasted_iota(jnp.int32, (BLK, 2 * BLK), 0)
     query_at = lax.rem(lax.broadcasted_iota(jnp.int32, (BLK, 2 * BLK), 1), BLK)
     tri[...] = jnp.where(key_at > query_at, MASKED, 0.0)
@@ -129,32 +169,6 @@
         starts.append(first)
 
     half = n_head // 2
-
-    def onward(d, o):
-        first = 2 * lax.rem(h // 2 + chips - d, chips)
-        return first >= n_head // 2, pltpu.make_async_remote_copy(
-            src_ref=kv.at[0, pl.ds(first, 2)], dst_ref=kv.at[o, pl.ds(first, 2)],
-            send_sem=c_send.at[o - 1, d], recv_sem=c_recv.at[o - 1, d],
-            device_id=after(o), device_id_type=MESH)
-
-    def each_part(o, act):
-        for d in range(chips):
-            late, copy = onward(d, o)
-            if o < 4:
-                act(copy)
-            else:
-                pl.when(late)(functools.partial(act, copy))
-
-    for d in (0, 1, 3, 2):
-        for e in (0, 1):
-            if (d, e) in heads_in:
-                heads_in[d, e].wait_recv()
-        for o in range(1, 5):
-            late, copy = onward(d, o)
-            if o < 4:
-                copy.start()
-            else:
-                pl.when(late)(copy.start)
 
     def prepare(t):
         if t < 4:
@@ -232,19 +246,12 @@
 
     out_order = (2, 1, 3, 0)
 
-    def back(d, o):
-        first = 2 * lax.rem(h // 2 + d, chips)
-        return first, pltpu.make_async_remote_copy(
-            src_ref=gsend.at[o, pl.ds(first, 2)], dst_ref=grecv.at[o, pl.ds(first, 2)],
-            send_sem=g_send.at[o - 1, d], recv_sem=g_recv.at[o - 1, d],
+    def back(o):
+        part = pl.ds(0, n_head) if o < 4 else pl.ds(half, half)
+        return pltpu.make_async_remote_copy(
+            src_ref=gsend.at[o, part], dst_ref=grecv.at[o, part],
+            send_sem=g_send.at[o - 1], recv_sem=g_recv.at[o - 1],
             device_id=before(o), device_id_type=MESH)
-
-    def each_back(d, o, act):
-        first, copy = back(d, o)
-        if o < 4:
-            act(copy)
-        else:
-            pl.when(first >= half)(functools.partial(act, copy))
 
     def send(o):
         if o < 4:
@@ -253,8 +260,7 @@
         else:
             gsend[4, half:, 0] = (dk_acc[4, :BLK] * SCALE).astype(BF).reshape(half, 32, DH)
             gsend[4, half:, 1] = dv_acc[4, :BLK].astype(BF).reshape(half, 32, DH)
-        for d in out_order:
-            each_back(d, o, lambda copy: copy.start())
+        back(o).start()
 
     grecv[4, :half] = jnp.zeros((half, 2, 32, DH), BF)
     close(1)
@@ -295,9 +301,9 @@
     lax.fori_loop(0, 2 * PAIRS, finish, 0, unroll=2)
 
     heads_out = []
+    for o in range(4, 0, -1):
+        back(o).wait_recv()
     for d in out_order:
-        for o in range(4, 0, -1):
-            each_back(d, o, lambda copy: copy.wait_recv())
         first = 2 * lax.rem(h // 2 + d, chips)
         part = pl.ds(first, 2)
         total = own[part]
@@ -320,9 +326,8 @@
         copy.wait_send()
     for o in range(1, 5):
         each_part(o, lambda copy: copy.wait_send())
-    for d in out_order:
-        for o in range(1, 5):
-            each_back(d, o, lambda copy: copy.wait_send())
+    for o in range(1, 5):
+        back(o).wait_send()
     for copy in heads_out:
         copy.wait()
     for j in range(n_head):
@@ -379,7 +384,7 @@
             pltpu.VMEM((n_head, 2, 32, DH), BF),
             dma((4,)),
             dma((7,)), dma((7,)), dma((4, 4)), dma((4, 4)),
-            dma((4, 4)), dma((4, 4)), dma((7,)), dma((7,)),
+            dma((4,)), dma((4,)), dma((7,)), dma((7,)),
         ],
         compiler_params=pltpu.CompilerParams(
             collective_id=0, has_side_effects=True, vmem_limit_bytes=56 * 2**20
@@ -392,7 +397,7 @@
         out_shape=tuple(jax.ShapeDtypeStruct(x.shape, BF) for x in (query, query, keys, keys)),
         in_specs=[vmem] * 4,
         out_specs=(hbm,) * 4,
-        scratch_shapes=[dma((4,))],
+        scratch_shapes=[dma((12,))],
     )(*(pltpu.with_memory_space_constraint(x, pltpu.VMEM) for x in held))
 
 

time: 50.8 us -> 50.2 us (0.988)
  Pallas kernels: 49.8 us -> 49 us
    pallas_call x1, Pallas kernels: 48.5 us -> 47.5 us  [local(): pl.pallas_call(functools.partial(kernel, n_ctx, n_head), name='attention'...]
where the time goes in v4:
time: 50.2 us; the launch traced here: 49.8 us
  Pallas kernels  49 us (98%)
  between operations  0.8 us (2%)
    pallas_call x1, Pallas kernels, local(): pl.pallas_call(functools.partial(kernel, n_ctx, n_head), name='attention'...  47.5 us
    pallas_call x1, Pallas kernels, local(): pl.pallas_call(write_out, name='write_out', out_shape=tuple((jax.ShapeDty...  1.46 us

profile of v4, /device:TPU:1, one launch (start us, length us, event | category | flops | bytes accessed | tf_op | source)
XLA Modules:
  0.0 49.8 jit_solution(10318897163749479655)
XLA Ops:
  0.6 47.5 %attention.1 = (bf16[256,2048]{1,0:T(8,128)(2,1)S(1)}, bf16[256,2048]{1,0:T(8,128)(2,1)S(1)}, bf16[32,1024]{1,0:T(8,128)(2,1)S(1)}, bf16[32,1024]{1,0:T(8,128)(2,1)S(1)}) custom-call(s32[16]{0:T(128)} %len_ref.1, bf16[256,2048]{1,0:T(8,128)(2,1)} %q_hbm.1, bf16[32,1024]{1,0:T(8,128)(2,1)} %k_hbm.1, bf16[32,1024]{1,0:T(8,128)(2,1)} %v_hbm.1, ...), custom_call_target="tpu_custom_call" | custom-call | flops 6499999744 | bytes 5242880 | tf_op jit(solution)/shard_map/attention/pallas_call | solution.py:346
  48.1 1.5 %write_out.1 = (bf16[256,2048]{1,0:T(8,128)(2,1)}, bf16[256,2048]{1,0:T(8,128)(2,1)}, bf16[32,1024]{1,0:T(8,128)(2,1)}, bf16[32,1024]{1,0:T(8,128)(2,1)}) custom-call(bf16[256,2048]{1,0:T(8,128)(2,1)S(1)} %get-tuple-element.8.refs_0_, bf16[256,2048]{1,0:T(8,128)(2,1)S(1)} %get-tuple-element.9.refs_1_, bf16[32,1024]{1,0:T(8,128)(2,1)S(1)} %get-tuple-element.10.refs_2_, ...), custom_call_target="tpu_custom_call" | custom-call | tf_op jit(solution)/shard_map/write_out/pallas_call | solution.py:394

commit v5 on v4

--- a/solution.py
+++ b/solution.py
@@ -53,7 +53,7 @@
     h = lax.axis_index("head")
 
     chips = n_head // 2
-    order = [(0, 1)] + [(d, e) for d in (1, 3, 2) for e in (0, 1)]
+    order = [(0, 1)] + [(d, e) for d in (2, 1, 3) for e in (0, 1)]
 
     def head_at(d, e):
         return 2 * lax.rem(h // 2 + d, chips) + lax.rem(h + e, 2)

time: 50.2 us -> 50.6 us (level)
  no operation moved by 1% of the time
where the time goes in v5:
time: 50.6 us; the launch traced here: 50.2 us
  Pallas kernels  49.4 us (98%)
  between operations  0.8 us (2%)
    pallas_call x1, Pallas kernels, local(): pl.pallas_call(functools.partial(kernel, n_ctx, n_head), name='attention'...  48 us
    pallas_call x1, Pallas kernels, local(): pl.pallas_call(write_out, name='write_out', out_shape=tuple((jax.ShapeDty...  1.46 us

profile of v5, /device:TPU:1, one launch (start us, length us, event | category | flops | bytes accessed | tf_op | source)
XLA Modules:
  0.0 50.2 jit_solution(9292819422099068011)
XLA Ops:
  0.6 48.0 %attention.1 = (bf16[256,2048]{1,0:T(8,128)(2,1)S(1)}, bf16[256,2048]{1,0:T(8,128)(2,1)S(1)}, bf16[32,1024]{1,0:T(8,128)(2,1)S(1)}, bf16[32,1024]{1,0:T(8,128)(2,1)S(1)}) custom-call(s32[16]{0:T(128)} %len_ref.1, bf16[256,2048]{1,0:T(8,128)(2,1)} %q_hbm.1, bf16[32,1024]{1,0:T(8,128)(2,1)} %k_hbm.1, bf16[32,1024]{1,0:T(8,128)(2,1)} %v_hbm.1, ...), custom_call_target="tpu_custom_call" | custom-call | flops 6499999744 | bytes 5242880 | tf_op jit(solution)/shard_map/attention/pallas_call | solution.py:346
  48.6 1.5 %write_out.1 = (bf16[256,2048]{1,0:T(8,128)(2,1)}, bf16[256,2048]{1,0:T(8,128)(2,1)}, bf16[32,1024]{1,0:T(8,128)(2,1)}, bf16[32,1024]{1,0:T(8,128)(2,1)}) custom-call(bf16[256,2048]{1,0:T(8,128)(2,1)S(1)} %get-tuple-element.8.refs_0_, bf16[256,2048]{1,0:T(8,128)(2,1)S(1)} %get-tuple-element.9.refs_1_, bf16[32,1024]{1,0:T(8,128)(2,1)S(1)} %get-tuple-element.10.refs_2_, ...), custom_call_target="tpu_custom_call" | custom-call | tf_op jit(solution)/shard_map/write_out/pallas_call | solution.py:394
